TPU v7x, 256 devices: a whole 4x4x8 slice. The times are simulated.
256 devices in a mesh: tm: 8 (over z), chan: 32 (over x, y, core).
Axes of the slice: x: 4, y: 4, z: 8, core: 2. Of those that a mesh axis runs over, the one named last changes fastest.
Arguments:
- voltages: bfloat16 [512, 1024, 2048], P('chan', None, 'tm'), may hold values from -4 to 4
- exponents: int32 [512, 16, 8], P('chan', None, 'tm'), may hold values from -2 to 2
- gain_real: float32 [512, 1024], P(None, 'chan'), may hold values from 0.1 to 1.9
- gain_imag: float32 [512, 1024], P(None, 'chan'), may hold values from -1.5 to 1.5
- delays: float32 [512, 256], replicated, may hold values from -8 to 8
- filter_taps: float32 [4, 1024], replicated, may hold values from -3 to 3
Outputs:
- beam_series: bfloat16 [256, 1024, 2048], P('chan', None, 'tm')
All inputs are finite; a program needn't handle non-finite values.
Results may differ from a plain program's by a relative error of at most 0.0062.
Values may be sent and summed in bfloat16 or wider, within the bound.
No kernel may reach another device: no remote copies, remote signals or barrier semaphores. Data moves between devices by JAX's collectives and lax.ppermute only.
A program may use at most 128 MiB of HBM per device.

v0:
```python
import math

import jax
import jax.numpy as jnp
from jax import lax
from jax.sharding import PartitionSpec as P

C = 1024


TWO_PI = 6.283185307179586


def from_behind(block, axis, distance):
    devices = range(lax.axis_size(axis))
    route = [(i - distance, i) for i in devices if i - distance in devices]
    return lax.ppermute(block, axis, route)


def inverse_tables(length):
    row_index = lax.broadcasted_iota(jnp.int32, (length, length), 0)
    col_index = lax.broadcasted_iota(jnp.int32, (length, length), 1)
    phases = TWO_PI / length * (row_index * col_index % length).astype(jnp.float32)
    normalizer = 1.0 / math.sqrt(length)
    cosine_table = (jnp.cos(phases) * normalizer).astype(jnp.bfloat16)
    sine_table = (jnp.sin(phases) * normalizer).astype(jnp.bfloat16)
    return (cosine_table, sine_table)


def beam_weights(gain_real, gain_imag, delays, chan_start):
    local_count = gain_real.shape[1]
    stations = delays.shape[0]
    channel = (chan_start + lax.broadcasted_iota(jnp.int32, (local_count,), 0)).astype(jnp.float32)
    frequency = (channel + 0.5) / C - 0.5
    turns = TWO_PI * frequency
    phases = turns[:, None, None] * jnp.transpose(delays)[None, :, :]
    cosines = jnp.cos(phases)
    sines = jnp.sin(phases)
    real_gain = jnp.transpose(gain_real)[:, None, :]
    imag_gain = jnp.transpose(gain_imag)[:, None, :]
    scale_factor = 1.0 / math.sqrt(stations)
    weight_real = (real_gain * cosines + imag_gain * sines) * scale_factor
    weight_imag = (imag_gain * cosines - real_gain * sines) * scale_factor
    return jnp.concatenate([weight_real, weight_imag], axis=1).astype(jnp.bfloat16)


def form_beams(weights, received):
    stations = received.shape[0]
    local_count = received.shape[1]
    frame_count = received.shape[3]
    flattened = received.reshape(stations, local_count, 2 * frame_count)
    product = jnp.einsum("cos,sck->cok", weights, flattened, preferred_element_type=jnp.float32)
    beam_count = weights.shape[1] // 2
    real_part = product[:, :beam_count, :frame_count] - product[:, beam_count:, frame_count:]
    imag_part = product[:, :beam_count, frame_count:] + product[:, beam_count:, :frame_count]
    return jnp.stack([real_part, imag_part], axis=2).astype(jnp.bfloat16)


def synthesize(cosine_table, sine_table, spectra):
    channels = spectra.shape[0]
    beams_local = spectra.shape[1]
    frame_count = spectra.shape[3]
    flattened = spectra.reshape(channels, beams_local, 2 * frame_count)
    cosine_part = jnp.einsum(
        "cn,cbk->bnk", cosine_table, flattened, preferred_element_type=jnp.float32
    )
    sine_part = jnp.einsum("cn,cbk->bnk", sine_table, flattened, preferred_element_type=jnp.float32)
    real_part = cosine_part[:, :, :frame_count] - sine_part[:, :, frame_count:]
    imag_part = sine_part[:, :, :frame_count] + cosine_part[:, :, frame_count:]
    return jnp.stack([real_part, imag_part], axis=2)


def apply_taps(filter_taps, extended, frame_count):
    tail_length = filter_taps.shape[0] - 1
    running = jnp.zeros(extended.shape[:3] + (frame_count,), jnp.float32)
    for tap_index in range(filter_taps.shape[0]):
        begin = tail_length - tap_index
        running = (
            running
            + filter_taps[tap_index][None, :, None, None]
            * extended[:, :, :, begin : begin + frame_count]
        )
    return running


def per_device(voltages, exponents, gain_real, gain_imag, delays, filter_taps):
    channels = voltages.shape[1]
    frame_count = voltages.shape[2] // 2
    block_width = channels // exponents.shape[1]
    factor = jnp.repeat(jnp.exp2(exponents.astype(jnp.float32)), block_width, axis=1).astype(
        jnp.bfloat16
    )
    scaled = voltages * factor
    local_count = gain_real.shape[1]
    weights = beam_weights(gain_real, gain_imag, delays, lax.axis_index("chan") * local_count)
    received = lax.all_to_all(scaled, "chan", split_axis=1, concat_axis=0, tiled=True)
    beamed = form_beams(weights, received.reshape(received.shape[0], local_count, 2, frame_count))
    spectra = lax.all_to_all(beamed, "chan", split_axis=1, concat_axis=0, tiled=True)
    cosine_table, sine_table = inverse_tables(channels)
    signal = synthesize(cosine_table, sine_table, spectra)
    tail_length = filter_taps.shape[0] - 1
    zeros_front = jnp.zeros(signal.shape[:3] + (tail_length,), jnp.float32)
    local_out = apply_taps(filter_taps, jnp.concatenate([zeros_front, signal], axis=3), frame_count)
    outgoing = apply_taps(
        filter_taps,
        jnp.concatenate([signal[:, :, :, frame_count - tail_length :], zeros_front], axis=3),
        tail_length,
    )
    incoming = from_behind(outgoing, "tm", 1)
    output = jnp.concatenate(
        [local_out[:, :, :, :tail_length] + incoming, local_out[:, :, :, tail_length:]], axis=3
    )
    return output.reshape(output.shape[0], channels, 2 * frame_count).astype(jnp.bfloat16)


def solution(mesh):
    placed = (
        P("chan", None, "tm"),
        P("chan", None, "tm"),
        P(None, "chan"),
        P(None, "chan"),
        P(),
        P(),
    )
    return jax.shard_map(
        per_device, mesh=mesh, in_specs=placed, out_specs=P("chan", None, "tm"), check_vma=False
    )
```

profile of v0, /device:TPU:128, one launch (start us, length us, event | category | flops | bytes accessed | tf_op | source)
XLA Modules:
  0.0 343.6 jit_solution(10548301587270115437)
XLA Ops:
  0.0 0.7 exponential_convert_fusion
  0.7 0.1 copy.37
  0.8 10.4 %copy_multiply_fusion = bf16[16,1024,256]{2,0,1:T(8,128)(2,1)} fusion(bf16[16,1024,256]{2,1,0:T(8,128)(2,1)} %param.6, bf16[16,1024]{0,1:T(8,128)(2,1)S(1)} %bitcast.42), kind=kLoop, calls=%fused_computation.20 | loop fusion | flops 4194304 | bytes 16809984 | tf_op jit(solution)/shard_map/mul | solution.py:93
  11.2 0.0 copy-start.2
  11.2 0.0 copy-start.3
  11.2 0.0 copy-start.4
  11.2 7.9 %all-to-all-start = ((bf16[16,1024,256]{2,0,1:T(8,128)(2,1)}), bf16[16,1024,256]{2,0,1:T(8,128)(2,1)}, u32[]{:S(2)}, u32[]{:S(2)}) async-start(bf16[16,1024,256]{2,0,1:T(8,128)(2,1)} %copy_multiply_fusion), calls=%async_computation | async-start | bytes 16777216 | tf_op jit(solution)/shard_map/all_to_all | solution.py:96
  19.1 0.0 copy-done.2
  19.1 0.2 copy.26
  19.3 0.0 copy-done.3
  19.4 0.0 copy-done.4
  19.4 65.9 %fusion.6 = (bf16[32,256,512]{2,1,0:T(8,128)(2,1)}, bf16[32,256,512]{2,1,0:T(8,128)(2,1)}) fusion(f32[32,512]{1,0:T(8,128)S(1)} %bitcast.44, f32[256,512]{1,0:T(8,128)S(1)} %copy.26, f32[32]{0:T(128)S(1)} %add_multiply_fusion, f32[32,512]{1,0:T(8,128)S(1)} %bitcast.45), kind=kLoop, calls=%fused_computation.8 | loop fusion | flops 46137344 | bytes 17432704 | tf_op jit(solution)/shard_map/convert.7
  85.3 47.4 %all-to-all-done = bf16[16,1024,256]{2,0,1:T(8,128)(2,1)} async-done(((bf16[16,1024,256]{2,0,1:T(8,128)(2,1)}), bf16[16,1024,256]{2,0,1:T(8,128)(2,1)}, u32[]{:S(2)}, u32[]{:S(2)}) %all-to-all-start) | async-done | bytes 8388640 | tf_op jit(solution)/shard_map/all_to_all | solution.py:96
  132.7 7.7 %copy.29 = bf16[16,32,32,256]{3,0,1,2:T(8,128)(2,1)} copy(bf16[16,32,32,256]{3,0,2,1:T(8,128)(2,1)} %bitcast.6) | data formatting | bytes 16777216 | tf_op jit(solution)/shard_map/all_to_all | solution.py:96
  140.4 14.3 %fusion.10 = f32[32,512,256]{2,1,0:T(8,128)} fusion(bf16[512,32,256]{2,0,1:T(8,128)(2,1)} %bitcast.41, bf16[32,256,512]{2,1,0:T(8,128)(2,1)} %get-tuple-element.10, bf16[32,256,512]{2,1,0:T(8,128)(2,1)} %get-tuple-element.9), kind=kOutput, calls=%fused_computation.12 | convolution fusion | flops 4328521728 | bytes 41943040 | tf_op jit(solution)/shard_map/cos,sck->cok/dot_general | solution.py:52
  154.7 6.7 %fusion.30 = (bf16[32,256,1,128]{3,1,0,2:T(8,128)(2,1)S(1)}, bf16[32,256,1,128]{3,1,0,2:T(8,128)(2,1)S(1)}) fusion(f32[32,512,256]{2,1,0:T(8,128)} %fusion.10), kind=kLoop, calls=%fused_computation.50 | loop fusion | flops 4194304 | bytes 20971520 | tf_op jit(solution)/shard_map/stack | solution.py:56
  161.4 0.4 pad_maximum_fusion.1
  161.8 4.7 %copy.30 = bf16[32,256,2,128]{3,0,2,1:T(8,128)(2,1)} copy(bf16[32,256,2,128]{3,1,0,2:T(8,128)(2,1)S(1)} %pad_maximum_fusion.1) | data formatting | bytes 8388608 | tf_op jit(solution)/shard_map/stack | solution.py:56
  166.5 0.0 copy-start.5
  166.5 16.5 %all-to-all-start.1 = ((bf16[32,256,2,128]{3,0,2,1:T(8,128)(2,1)}), bf16[32,256,2,128]{3,0,2,1:T(8,128)(2,1)}, u32[]{:S(2)}, u32[]{:S(2)}) async-start(bf16[32,256,2,128]{3,0,2,1:T(8,128)(2,1)} %copy.30), calls=%async_computation.1 | async-start | bytes 8388608 | tf_op jit(solution)/shard_map/all_to_all | solution.py:98
  183.0 0.0 copy-done.5
  183.0 52.7 %all-to-all-done.1 = bf16[32,256,2,128]{3,0,2,1:T(8,128)(2,1)} async-done(((bf16[32,256,2,128]{3,0,2,1:T(8,128)(2,1)}), bf16[32,256,2,128]{3,0,2,1:T(8,128)(2,1)}, u32[]{:S(2)}, u32[]{:S(2)}) %all-to-all-start.1) | async-done | bytes 4194336 | tf_op jit(solution)/shard_map/all_to_all | solution.py:98
  235.7 12.3 %copy.32 = bf16[32,32,8,2,128]{4,2,3,1,0:T(8,128)(2,1)} copy(bf16[32,32,8,2,128]{4,1,3,2,0:T(8,128)(2,1)} %bitcast.13) | data formatting | bytes 8388608 | tf_op jit(solution)/shard_map/all_to_all | solution.py:98
  248.1 6.7 %copy.33 = bf16[1024,8,256]{0,2,1:T(8,128)(2,1)} copy(bf16[1024,8,256]{2,1,0:T(8,128)(2,1)} %bitcast.39) | data formatting | bytes 8388608 | tf_op jit(solution)/shard_map/reshape | solution.py:63
  254.8 0.0 copy-start.1
  254.8 22.7 %convolution_bitcast_fusion = f32[8,1024,256]{1,2,0:T(8,128)} fusion(bf16[1024,8,256]{0,2,1:T(8,128)(2,1)} %copy.33), kind=kOutput, calls=%fused_computation.46 | convolution fusion | flops 4311744512 | bytes 12582912 | tf_op jit(solution)/shard_map/cn,cbk->bnk/dot_general | solution.py:67
  277.5 0.0 copy-done.1
  277.5 20.4 %convolution_bitcast_fusion.1 = f32[8,1024,256]{1,2,0:T(8,128)} fusion(bf16[1024,8,256]{0,2,1:T(8,128)(2,1)S(1)} %copy-done.1), kind=kOutput, calls=%fused_computation.47 | convolution fusion | flops 4311744512 | bytes 12582912 | tf_op jit(solution)/shard_map/cn,cbk->bnk/dot_general | solution.py:64
  297.9 10.4 %fusion.20 = (f32[8,1024,1,128]{1,3,0,2:T(8,128)S(1)}, f32[8,1024,1,128]{1,3,0,2:T(8,128)}) fusion(f32[8,1024,256]{1,2,0:T(8,128)} %convolution_bitcast_fusion, f32[8,1024,256]{1,2,0:T(8,128)} %convolution_bitcast_fusion.1), kind=kLoop, calls=%fused_computation.34 | loop fusion | flops 2097152 | bytes 25165824 | tf_op jit(solution)/shard_map/stack | solution.py:70
  308.3 0.0 copy-start
  308.3 6.8 %pad_maximum_fusion = f32[8,1024,2,128]{1,3,0,2:T(8,128)} fusion(f32[8,1024,1,128]{1,3,0,2:T(8,128)} %get-tuple-element.6, f32[8,1024,1,128]{1,3,0,2:T(8,128)S(1)} %get-tuple-element.5), kind=kLoop, calls=%fused_computation.17 | loop fusion | flops 2097152 | bytes 16777216 | tf_op jit(solution)/shard_map/stack | solution.py:70
  315.1 0.0 copy-done
  315.1 0.1 fusion.36
  315.1 0.2 fusion.40
  315.3 2.9 collective-permute-start
  318.3 13.0 %multiply_add_fusion = f32[8,1024,2,128]{1,3,0,2:T(8,128)S(1)} fusion(f32[8,1024,2,128]{1,3,0,2:T(8,128)} %pad_maximum_fusion, f32[1024]{0:T(1024)S(1)} %bitcast.49, f32[1024]{0:T(1024)S(1)} %bitcast.51, f32[1024]{0:T(1024)S(1)} %bitcast.47, f32[1024]{0:T(1024)S(1)} %bitcast.53), kind=kLoop, calls=%fused_computation.21 | loop fusion | flops 14680064 | bytes 16793600 | tf_op jit(solution)/shard_map/add | solution.py:79
  331.2 1.3 slice.154
  332.5 0.0 collective-permute-done
  332.6 0.1 fusion.42
  332.6 1.9 pad_maximum_fusion.2
  334.5 2.4 copy.35
  336.9 6.4 %copy.36 = bf16[8,1024,256]{2,1,0:T(8,128)(2,1)} copy(bf16[8,1024,256]{1,2,0:T(8,128)(2,1)} %bitcast.40) | data formatting | bytes 8388608 | tf_op jit(solution)/shard_map/convert_element_type | solution.py:113
  (4 shorter events, 0.1 us)
Async XLA Ops:
  11.2 7.9 %copy-start.2 = (f32[512,256]{1,0:T(8,128)S(1)}, f32[512,256]{1,0:T(8,128)}, u32[]{:S(2)}) copy-start(f32[512,256]{1,0:T(8,128)} %param.10) | copy-start | bytes 1572868
  11.2 8.1 %copy-start.3 = (f32[512,32]{0,1:T(8,128)S(1)}, f32[512,32]{0,1:T(8,128)}, u32[]{:S(2)}) copy-start(f32[512,32]{0,1:T(8,128)} %param.9) | copy-start | bytes 196612
  11.2 8.1 %copy-start.4 = (f32[512,32]{0,1:T(8,128)S(1)}, f32[512,32]{0,1:T(8,128)}, u32[]{:S(2)}) copy-start(f32[512,32]{0,1:T(8,128)} %param.8) | copy-start | bytes 196612
  11.2 121.4 %all-to-all-start = ((bf16[16,1024,256]{2,0,1:T(8,128)(2,1)}), bf16[16,1024,256]{2,0,1:T(8,128)(2,1)}, u32[]{:S(2)}, u32[]{:S(2)}) async-start(bf16[16,1024,256]{2,0,1:T(8,128)(2,1)} %copy_multiply_fusion), calls=%async_computation | async-start | bytes 16777216 | tf_op jit(solution)/shard_map/all_to_all | solution.py:96
  166.5 16.5 %copy-start.5 = (f32[4,1024]{1,0:T(4,128)S(1)}, f32[4,1024]{1,0:T(4,128)}, u32[]{:S(2)}) copy-start(f32[4,1024]{1,0:T(4,128)} %param.11) | copy-start | bytes 49156
  166.5 69.2 %all-to-all-start.1 = ((bf16[32,256,2,128]{3,0,2,1:T(8,128)(2,1)}), bf16[32,256,2,128]{3,0,2,1:T(8,128)(2,1)}, u32[]{:S(2)}, u32[]{:S(2)}) async-start(bf16[32,256,2,128]{3,0,2,1:T(8,128)(2,1)} %copy.30), calls=%async_computation.1 | async-start | bytes 8388608 | tf_op jit(solution)/shard_map/all_to_all | solution.py:98
  254.8 22.7 %copy-start.1 = (bf16[1024,8,256]{0,2,1:T(8,128)(2,1)S(1)}, bf16[1024,8,256]{0,2,1:T(8,128)(2,1)}, u32[]{:S(2)}) copy-start(bf16[1024,8,256]{0,2,1:T(8,128)(2,1)} %copy.33) | copy-start | bytes 12582916
  308.3 6.8 %copy-start = (f32[8,1024,1,128]{1,3,0,2:T(8,128)S(1)}, f32[8,1024,1,128]{1,3,0,2:T(8,128)}, u32[]{:S(2)}) copy-start(f32[8,1024,1,128]{1,3,0,2:T(8,128)} %get-tuple-element.6) | copy-start | bytes 12582916
  315.3 17.2 %collective-permute-start = (f32[8,1024,2,3]{1,3,0,2:T(4,128)S(1)}, f32[8,1024,2,3]{1,3,0,2:T(4,128)S(1)}, u32[]{:S(2)}, u32[]{:S(2)}) collective-permute-start(f32[8,1024,2,3]{1,3,0,2:T(4,128)S(1)} %fusion.40), channel_id=1, source_target_pairs={{0,32},{32,64},{64,96},{96,128},{128,160},{160,192},{192,224},{1,3... | collective-permute-start | bytes 589832 | tf_op jit(solution)/shard_map/ppermute | solution.py:17
where the time goes:
time: 350 us; the launch traced here: 344 us
  other arithmetic  116 us (33%)
  waiting for transfers between devices  100 us (29%)
  matrix products  57.4 us (16%)
  local copies, waits for them, and re-layouts  42 us (12%)
  starting transfers between devices  27.3 us (8%)
    another operation x2, other arithmetic  66 us
    all_to_all x1, waiting for transfers between devices, per_device(): lax.all_to_all(beamed, 'chan', split_axis=1, concat_axis=0, tiled=True)  52.7 us
    all_to_all x1, waiting for transfers between devices, per_device(): lax.all_to_all(scaled, 'chan', split_axis=1, concat_axis=0, tiled=True)  47.4 us
    dot_general x1, matrix products, synthesize(): jnp.einsum('cn,cbk->bnk', sine_table, flattened, preferred_element_type=j...  22.7 us
    dot_general x1, matrix products, synthesize(): jnp.einsum('cn,cbk->bnk', cosine_table, flattened, preferred_element_type...  20.4 us
    another operation x3, other arithmetic, synthesize(): return jnp.stack([real_part, imag_part], axis=2)  17.2 us
    all_to_all x1, starting transfers between devices, per_device(): lax.all_to_all(beamed, 'chan', split_axis=1, concat_axis=0, tiled=True)  16.5 us
    dot_general x1, matrix products, form_beams(): jnp.einsum('cos,sck->cok', weights, flattened, preferred_element_type=jnp...  14.3 us
  transfers between devices with their start and end apart: 3, of which 2 were waited for; matrix products, arithmetic and copies ran while one was open for 23% of the time, Pallas kernels for 0%

commit v1 on v0

v1 whole, which is shorter than its diff:
```python
import math

import jax
import jax.numpy as jnp
from jax import lax
from jax.experimental import pallas as pl
from jax.experimental.pallas import tpu as pltpu
from jax.sharding import PartitionSpec as P

C = 1024
TAPS = 4
TILE = 16
FR = 128
TWO_PI = 6.283185307179586


def swap_matrix():
    row = lax.broadcasted_iota(jnp.int32, (256, 256), 0)
    col = lax.broadcasted_iota(jnp.int32, (256, 256), 1)
    hit = (row // TILE == col % TILE) & (row % TILE == col // TILE)
    return jnp.where(hit, 1.0, 0.0).astype(jnp.bfloat16)


def parity_table(parity):
    sample = lax.broadcasted_iota(jnp.int32, (C // 2, C // 2), 0)
    channel = 2 * lax.broadcasted_iota(jnp.int32, (C // 2, C // 2), 1) + parity
    phases = TWO_PI / C * (sample * channel % C).astype(jnp.float32)
    normalizer = 1.0 / math.sqrt(C)
    cosines = (jnp.cos(phases) * normalizer).astype(jnp.bfloat16)
    sines = (jnp.sin(phases) * normalizer).astype(jnp.bfloat16)
    return jnp.concatenate([cosines, sines], axis=0)


def beam_weights(gain_real, gain_imag, delays, chan_start):
    local_count = gain_real.shape[1]
    stations = delays.shape[0]
    channel = (chan_start + lax.broadcasted_iota(jnp.int32, (local_count,), 0)).astype(jnp.float32)
    frequency = (channel + 0.5) / C - 0.5
    turns = TWO_PI * frequency
    phases = turns[:, None, None] * jnp.transpose(delays)[None, :, :]
    cosines = jnp.cos(phases)
    sines = jnp.sin(phases)
    real_gain = jnp.transpose(gain_real)[:, None, :]
    imag_gain = jnp.transpose(gain_imag)[:, None, :]
    scale_factor = 1.0 / math.sqrt(stations)
    weight_real = (real_gain * cosines + imag_gain * sines) * scale_factor
    weight_imag = (imag_gain * cosines - real_gain * sines) * scale_factor
    return weight_real.astype(jnp.bfloat16), weight_imag.astype(jnp.bfloat16)


SC_STEP = 128
CB = 64


def scale_kernel(exp_ref, volt_ref, out_ref, perm_ref):
    step = pl.program_id(0)

    @pl.when(step == 0)
    def _():
        perm_ref[...] = swap_matrix()

    station = lax.broadcasted_iota(jnp.int32, (TILE, 2 * FR), 0)
    for block in range(SC_STEP // CB):
        power = jnp.zeros((TILE, 2 * FR), jnp.int32)
        for s in range(TILE):
            power = jnp.where(station == s, exp_ref[s, step * (SC_STEP // CB) + block], power)
        factor = jnp.exp2(power.astype(jnp.float32)).astype(jnp.bfloat16).astype(jnp.float32)
        for part in range(CB // TILE):
            start = block * CB + part * TILE
            rows = volt_ref[:, start : start + TILE, :].reshape(256, 2 * FR)
            moved = jnp.dot(perm_ref[...], rows, preferred_element_type=jnp.float32)
            scaled = moved.reshape(TILE, TILE, 2 * FR) * factor[None]
            out_ref[start : start + TILE] = scaled.astype(jnp.bfloat16)


def scale_and_turn(voltages, exponents):
    return pl.pallas_call(
        scale_kernel,
        grid=(C // SC_STEP,),
        in_specs=[
            pl.BlockSpec(memory_space=pltpu.SMEM),
            pl.BlockSpec((TILE, SC_STEP, 2 * FR), lambda i: (0, i, 0)),
        ],
        out_specs=pl.BlockSpec((SC_STEP, TILE, 2 * FR), lambda i: (i, 0, 0)),
        out_shape=jax.ShapeDtypeStruct((C, TILE, 2 * FR), jnp.bfloat16),
        scratch_shapes=[pltpu.VMEM((256, 256), jnp.bfloat16)],
        compiler_params=pltpu.CompilerParams(vmem_limit_bytes=24 * 2**20),
        name="scale",
    )(exponents, voltages)


BF_STEP = 2


def beam_kernel(wr_ref, wi_ref, x_ref, out_ref, perm_ref, beams_ref):
    q, j = pl.program_id(0), pl.program_id(1)

    @pl.when((q == 0) & (j == 0))
    def _():
        perm_ref[...] = swap_matrix()

    for i in range(BF_STEP):
        x = x_ref[:, i, 0].reshape(512, 2 * FR)
        pr = jnp.dot(wr_ref[i, 0], x, preferred_element_type=jnp.float32)
        pi = jnp.dot(wi_ref[i, 0], x, preferred_element_type=jnp.float32)
        real = pr[:, :FR] - pi[:, FR:]
        imag = pr[:, FR:] + pi[:, :FR]
        beams_ref[j * BF_STEP + i, :, :FR] = real.astype(jnp.bfloat16)
        beams_ref[j * BF_STEP + i, :, FR:] = imag.astype(jnp.bfloat16)

    @pl.when(j == pl.num_programs(1) - 1)
    def _():
        for group in range(256 // TILE):
            rows = beams_ref[:, group * TILE : (group + 1) * TILE, :].reshape(256, 2 * FR)
            moved = jnp.dot(perm_ref[...], rows, preferred_element_type=jnp.float32)
            out_ref[group * TILE : (group + 1) * TILE, 0] = moved.reshape(
                TILE, TILE, 2 * FR
            ).astype(jnp.bfloat16)


def form_beams(weight_real, weight_imag, received):
    weight_spec = pl.BlockSpec((BF_STEP, 1, 256, 512), lambda q, j: (j, q, 0, 0))
    return pl.pallas_call(
        beam_kernel,
        grid=(2, 16 // BF_STEP),
        in_specs=[
            weight_spec,
            weight_spec,
            pl.BlockSpec((32, BF_STEP, 1, TILE, 2 * FR), lambda q, j: (0, j, q, 0, 0)),
        ],
        out_specs=pl.BlockSpec((256, 1, TILE, 2 * FR), lambda q, j: (0, q, 0, 0)),
        out_shape=jax.ShapeDtypeStruct((256, 2, TILE, 2 * FR), jnp.bfloat16),
        scratch_shapes=[
            pltpu.VMEM((256, 256), jnp.bfloat16),
            pltpu.VMEM((16, 256, 2 * FR), jnp.bfloat16),
        ],
        compiler_params=pltpu.CompilerParams(vmem_limit_bytes=32 * 2**20),
        name="beamform",
    )(
        weight_real.reshape(16, 2, 256, 512),
        weight_imag.reshape(16, 2, 256, 512),
        received.reshape(32, 16, 2, TILE, 2 * FR),
    )


HALF = C // 2
ROWS = 64


def synth_kernel(te_ref, to_ref, taps_ref, ptaps_ref, y_ref, out_ref, tail_ref, even_ref, odd_ref, pack_ref):
    beam = pl.program_id(0)
    even = y_ref[:, 0, 0].reshape(HALF, 2 * FR)
    odd = y_ref[:, 0, 1].reshape(HALF, 2 * FR)
    even_ref[...] = jnp.dot(te_ref[...], even, preferred_element_type=jnp.float32)
    odd_ref[...] = jnp.dot(to_ref[...], odd, preferred_element_type=jnp.float32)
    lane = lax.broadcasted_iota(jnp.int32, (ROWS, FR), 1)
    slot = lane // 4
    for r in range(0, HALF, ROWS):
        cos_rows, sin_rows = pl.ds(r, ROWS), pl.ds(HALF + r, ROWS)
        parts = []
        for ref in (even_ref, odd_ref):
            real = ref[cos_rows, :FR] - ref[sin_rows, FR:]
            imag = ref[sin_rows, :FR] + ref[cos_rows, FR:]
            parts.append((real, imag))
        packed = pack_ref[cos_rows, :]
        for n1 in range(2):
            for ri in range(2):
                a, b = parts[0][ri], parts[1][ri]
                signal = a + b if n1 == 0 else a - b
                total = taps_ref[0, pl.ds(n1 * HALF + r, ROWS), :] * signal
                for k in range(1, TAPS):
                    shifted = jnp.where(lane >= k, pltpu.roll(signal, k, 1), 0.0)
                    total += taps_ref[k, pl.ds(n1 * HALF + r, ROWS), :] * shifted
                out_ref[0, pl.ds(n1 * HALF + r, ROWS), ri * FR : (ri + 1) * FR] = total.astype(
                    jnp.bfloat16
                )
                where = beam * 4 + n1 * 2 + ri
                packed = jnp.where(slot == where, pltpu.roll(signal, (where * 4 + 4) % FR, 1), packed)
        pack_ref[cos_rows, :] = packed

    @pl.when(beam == pl.num_programs(0) - 1)
    def _():
        for r in range(0, HALF, ROWS):
            rows = pl.ds(r, ROWS)
            packed = pack_ref[rows, :]
            total = jnp.zeros((ROWS, FR), jnp.float32)
            for k in range(1, TAPS):
                moved = jnp.where(lane % 4 < k, pltpu.roll(packed, FR - (4 - k), 1), 0.0)
                total += ptaps_ref[k - 1, rows, :] * moved
            tail_ref[rows, :] = total.astype(jnp.bfloat16)


def synthesize(table_even, table_odd, wide_taps, packed_taps, received):
    whole = pl.BlockSpec(memory_space=pltpu.VMEM)
    return pl.pallas_call(
        synth_kernel,
        grid=(8,),
        in_specs=[
            whole,
            whole,
            whole,
            whole,
            pl.BlockSpec((32, 1, 2, TILE, 2 * FR), lambda b: (0, b, 0, 0, 0)),
        ],
        out_specs=[
            pl.BlockSpec((1, C, 2 * FR), lambda b: (b, 0, 0)),
            pl.BlockSpec((HALF, FR), lambda b: (0, 0)),
        ],
        out_shape=[
            jax.ShapeDtypeStruct((8, C, 2 * FR), jnp.bfloat16),
            jax.ShapeDtypeStruct((HALF, FR), jnp.bfloat16),
        ],
        scratch_shapes=[
            pltpu.VMEM((C, 2 * FR), jnp.float32),
            pltpu.VMEM((C, 2 * FR), jnp.float32),
            pltpu.VMEM((HALF, FR), jnp.float32),
        ],
        compiler_params=pltpu.CompilerParams(vmem_limit_bytes=32 * 2**20),
        name="synthesis",
    )(table_even, table_odd, wide_taps, packed_taps, received)


def patch_kernel(in_ref, series_ref, out_ref):
    beam = pl.program_id(0)
    lane = lax.broadcasted_iota(jnp.int32, (ROWS, FR), 1)
    for r in range(0, HALF, ROWS):
        incoming = in_ref[pl.ds(r, ROWS), :].astype(jnp.float32)
        for n1 in range(2):
            for ri in range(2):
                where = beam * 4 + n1 * 2 + ri
                head = jnp.where(lane < TAPS - 1, pltpu.roll(incoming, (FR - where * 4) % FR, 1), 0.0)
                rows, cols = pl.ds(n1 * HALF + r, ROWS), slice(ri * FR, (ri + 1) * FR)
                old = series_ref[0, rows, cols].astype(jnp.float32)
                out_ref[0, rows, cols] = (old + head).astype(jnp.bfloat16)


def patch(incoming, series):
    block = pl.BlockSpec((1, C, 2 * FR), lambda b: (b, 0, 0))
    return pl.pallas_call(
        patch_kernel,
        grid=(8,),
        in_specs=[
            pl.BlockSpec(memory_space=pltpu.VMEM),
            block,
        ],
        out_specs=block,
        out_shape=jax.ShapeDtypeStruct((8, C, 2 * FR), jnp.bfloat16),
        input_output_aliases={1: 0},
        compiler_params=pltpu.CompilerParams(vmem_limit_bytes=16 * 2**20),
        name="patch",
    )(incoming, series)


def per_device(voltages, exponents, gain_real, gain_imag, delays, filter_taps):
    local_count = gain_real.shape[1]
    turned = scale_and_turn(voltages, exponents.reshape(TILE, -1))
    received = lax.all_to_all(turned, "chan", split_axis=0, concat_axis=0, tiled=True)
    weight_real, weight_imag = beam_weights(
        gain_real, gain_imag, delays, lax.axis_index("chan") * local_count
    )
    beamed = form_beams(weight_real, weight_imag, received)
    spectra = lax.all_to_all(beamed, "chan", split_axis=0, concat_axis=0, tiled=True)
    wide_taps = jnp.broadcast_to(filter_taps[:, :, None], (TAPS, C, FR))
    by_half = filter_taps[1:].reshape(TAPS - 1, 2, HALF)
    n1_of_lane = (lax.broadcasted_iota(jnp.int32, (FR,), 0) // 8) % 2
    packed_taps = jnp.where(n1_of_lane == 0, by_half[:, 0, :, None], by_half[:, 1, :, None])
    series, tail = synthesize(
        parity_table(0),
        parity_table(1),
        wide_taps,
        packed_taps,
        spectra.reshape(32, 8, 2, TILE, 2 * FR),
    )
    groups = lax.axis_size("tm")
    incoming = lax.ppermute(tail, "tm", [(g, g + 1) for g in range(groups - 1)])
    return patch(incoming, series)


def solution(mesh):
    placed = (
        P("chan", None, "tm"),
        P("chan", None, "tm"),
        P(None, "chan"),
        P(None, "chan"),
        P(),
        P(),
    )
    return jax.shard_map(
        per_device, mesh=mesh, in_specs=placed, out_specs=P("chan", None, "tm"), check_vma=False
    )
```

time: 350 us -> 262 us (0.75)
  matrix products: 57.4 us -> 0 us
  Pallas kernels: 0 us -> 43.5 us
  other arithmetic: 116 us -> 75.5 us
  local copies, waits for them, and re-layouts: 42 us -> 17 us
  waiting for transfers between devices: 100 us -> 95.8 us
    another operation x7 -> x0, other arithmetic: 90.3 us -> none
    convert_element_type x1 -> x3, other arithmetic: 0.72 us -> 74.8 us  [the longest x1 65.9 us: beam_weights(): return (weight_real.astype(jnp.bfloat16), weight_imag.astype(jnp.bfloat16))]
    dot_general x3 -> x0, matrix products: 57.4 us -> none  [the longest x1 22.7 us: synthesize(): jnp.einsum('cn,cbk->bnk', sine_table, flattened, preferred_element_type=j...]
    pallas_call x0 -> x4, Pallas kernels: none -> 43.5 us  [the longest x1 16 us: synthesize(): pl.pallas_call(synth_kernel, grid=(8,), in_specs=[whole, whole, whole, wh...]
    all_to_all x2 -> x0, local copies, waits for them, and re-layouts: 20 us -> none  [the longest x1 12.3 us: per_device(): lax.all_to_all(beamed, 'chan', split_axis=1, concat_axis=0, tiled=True)]
    unnamed x12 -> x20, local copies, waits for them, and re-layouts: 0.02 us -> 16.1 us
    add x2 -> x1, other arithmetic: 13.2 us -> 0.01 us  [parity_table(): channel = 2 * lax.broadcasted_iota(jnp.int32, (C // 2, C // 2), 1) + parity]
    mul x2 -> x1, other arithmetic: 10.4 us -> 0.01 us  [parity_table(): channel = 2 * lax.broadcasted_iota(jnp.int32, (C // 2, C // 2), 1) + parity]
  transfers between devices with their start and end apart: 3 -> 3, of which waited for: 2 -> 3; matrix products, arithmetic and copies ran while one was open for 23% -> 29% of each run, Pallas kernels for 0% -> 0%
where the time goes in v1:
time: 262 us; the launch traced here: 259 us
  waiting for transfers between devices  95.8 us (37%)
  other arithmetic  75.5 us (29%)
  Pallas kernels  43.5 us (17%)
  starting transfers between devices  27 us (10%)
  local copies, waits for them, and re-layouts  17 us (6%)
    convert_element_type x1, other arithmetic, beam_weights(): return (weight_real.astype(jnp.bfloat16), weight_imag.astype(jnp.bfloat16))  65.9 us
    all_to_all x1, waiting for transfers between devices, per_device(): lax.all_to_all(turned, 'chan', split_axis=0, concat_axis=0, tiled=True)  47.5 us
    all_to_all x1, waiting for transfers between devices, per_device(): lax.all_to_all(beamed, 'chan', split_axis=0, concat_axis=0, tiled=True)  43.1 us
    all_to_all x1, starting transfers between devices, per_device(): lax.all_to_all(beamed, 'chan', split_axis=0, concat_axis=0, tiled=True)  16.5 us
    unnamed x20, local copies, waits for them, and re-layouts  16.1 us
    pallas_call x1, Pallas kernels, synthesize(): pl.pallas_call(synth_kernel, grid=(8,), in_specs=[whole, whole, whole, wh...  16 us
    pallas_call x1, Pallas kernels, form_beams(): pl.pallas_call(beam_kernel, grid=(2, 16 // BF_STEP), in_specs=[weight_spe...  15.2 us
    convert_element_type x2, other arithmetic, parity_table(): cosines = (jnp.cos(phases) * normalizer).astype(jnp.bfloat16)  8.97 us
  transfers between devices with their start and end apart: 3, of which 3 were waited for; matrix products, arithmetic and copies ran while one was open for 29% of the time, Pallas kernels for 0%

profile of v1, /device:TPU:128, one launch (start us, length us, event | category | flops | bytes accessed | tf_op | source)
XLA Modules:
  0.0 258.9 jit_solution(15549099951066655381)
XLA Ops:
  0.0 0.0 copy-start.4
  0.0 3.4 %copy-done.4 = bf16[16,1024,256]{2,1,0:T(8,128)(2,1)S(1)} copy-done((bf16[16,1024,256]{2,1,0:T(8,128)(2,1)S(1)}, bf16[16,1024,256]{2,1,0:T(8,128)(2,1)}, u32[]{:S(2)}) %copy-start.4) | copy-done | bytes 8388632
  3.4 0.0 copy-start.5
  3.4 0.7 copy-done.5
  4.1 4.9 %scale.1 = bf16[1024,16,256]{2,1,0:T(8,128)(2,1)S(1)} custom-call(s32[16,16]{1,0:T(8,128)S(1)} %bitcast.11, bf16[16,1024,256]{2,1,0:T(8,128)(2,1)S(1)} %copy-done.4), custom_call_target="tpu_custom_call" | custom-call | tf_op jit(solution)/shard_map/scale/pallas_call | solution.py:77
  9.0 0.0 copy-start.2
  9.0 3.2 %copy-done.2 = bf16[1024,16,256]{2,1,0:T(8,128)(2,1)} copy-done((bf16[1024,16,256]{2,1,0:T(8,128)(2,1)}, bf16[1024,16,256]{2,1,0:T(8,128)(2,1)S(1)}, u32[]{:S(2)}) %copy-start.2) | copy-done | bytes 8388632
  12.2 0.0 copy-start.8
  12.2 0.0 copy-start.9
  12.2 0.0 copy-start.6
  12.2 7.6 %all-to-all-start = ((bf16[1024,16,256]{2,1,0:T(8,128)(2,1)}), bf16[1024,16,256]{2,1,0:T(8,128)(2,1)}, u32[]{:S(2)}, u32[]{:S(2)}) async-start(bf16[1024,16,256]{2,1,0:T(8,128)(2,1)} %copy-done.2), calls=%async_computation | async-start | bytes 16777216 | tf_op jit(solution)/shard_map/all_to_all | solution.py:257
  19.8 0.0 copy-done.8
  19.9 0.0 copy-done.9
  19.9 0.0 copy-done.6
  19.9 0.2 copy.10
  20.1 65.9 %fusion.9 = (bf16[16,2,256,512]{3,2,1,0:T(8,128)(2,1)}, bf16[16,2,256,512]{3,2,1,0:T(8,128)(2,1)}) fusion(f32[16,2,512]{2,1,0:T(2,128)S(1)} %mul.133, f32[256,512]{1,0:T(8,128)S(1)} %copy.10, f32[16,2]{1,0:T(8,128)S(1)} %add_multiply_fusion, f32[16,2,512]{2,1,0:T(2,128)S(1)} %mul.124), kind=kLoop, calls=%fused_computation.11 | loop fusion | flops 46137344 | bytes 17432704 | tf_op jit(solution)/shard_map/convert_element_type | solution.py:48
  86.0 47.5 %all-to-all-done = bf16[1024,16,256]{2,1,0:T(8,128)(2,1)} async-done(((bf16[1024,16,256]{2,1,0:T(8,128)(2,1)}), bf16[1024,16,256]{2,1,0:T(8,128)(2,1)}, u32[]{:S(2)}, u32[]{:S(2)}) %all-to-all-start) | async-done | bytes 8388640 | tf_op jit(solution)/shard_map/all_to_all | solution.py:257
  133.5 0.0 copy-start
  133.5 3.4 %copy-done = bf16[16,2,256,512]{3,2,1,0:T(8,128)(2,1)S(1)} copy-done((bf16[16,2,256,512]{3,2,1,0:T(8,128)(2,1)S(1)}, bf16[16,2,256,512]{3,2,1,0:T(8,128)(2,1)}, u32[]{:S(2)}) %copy-start) | copy-done | bytes 8388632
  136.9 0.0 copy-start.1
  136.9 3.4 %copy-done.1 = bf16[16,2,256,512]{3,2,1,0:T(8,128)(2,1)S(1)} copy-done((bf16[16,2,256,512]{3,2,1,0:T(8,128)(2,1)S(1)}, bf16[16,2,256,512]{3,2,1,0:T(8,128)(2,1)}, u32[]{:S(2)}) %copy-start.1) | copy-done | bytes 8388632
  140.3 15.2 %beamform.1 = bf16[256,2,16,256]{3,2,1,0:T(8,128)(2,1)S(1)} custom-call(bf16[16,2,256,512]{3,2,1,0:T(8,128)(2,1)S(1)} %copy-done.1, bf16[16,2,256,512]{3,2,1,0:T(8,128)(2,1)S(1)} %copy-done, bf16[32,16,2,16,256]{4,3,2,1,0:T(8,128)(2,1)} %bitcast.7.x_ref), custom_call_target="tpu_custom_call" | custom-call | tf_op jit(solution)/shard_map/beamform/pallas_call | solution.py:123
  155.5 0.0 copy-start.3
  155.5 2.0 copy-done.3
  157.5 0.0 copy-start.7
  157.5 16.5 %all-to-all-start.1 = ((bf16[256,2,16,256]{3,2,1,0:T(8,128)(2,1)}), bf16[256,2,16,256]{3,2,1,0:T(8,128)(2,1)}, u32[]{:S(2)}, u32[]{:S(2)}) async-start(bf16[256,2,16,256]{3,2,1,0:T(8,128)(2,1)} %copy-done.3), calls=%async_computation.1 | async-start | bytes 8388608 | tf_op jit(solution)/shard_map/all_to_all | solution.py:262
  174.0 0.0 copy-done.7
  174.0 4.5 %multiply_convert_fusion.3 = (bf16[512,512]{1,0:T(8,128)(2,1)S(1)}, bf16[512,512]{1,0:T(8,128)(2,1)S(1)}) fusion(s32[512]{0:T(512)S(1)} %iota_multiply_fusion), kind=kLoop, calls=%fused_computation.31 | loop fusion | flops 4718592 | bytes 1050624 | tf_op jit(solution)/shard_map/convert_element_type | solution.py:29
  178.5 4.5 %multiply_convert_fusion.1 = (bf16[512,512]{1,0:T(8,128)(2,1)S(1)}, bf16[512,512]{1,0:T(8,128)(2,1)S(1)}) fusion(s32[512]{0:T(512)S(1)} %broadcast_add_fusion), kind=kLoop, calls=%fused_computation.27 | loop fusion | flops 4718592 | bytes 1050624 | tf_op jit(solution)/shard_map/convert_element_type | solution.py:29
  183.0 0.1 pad_maximum_fusion
  183.2 0.5 broadcast_select_fusion.ptaps_ref
  183.6 43.1 %all-to-all-done.1 = bf16[256,2,16,256]{3,2,1,0:T(8,128)(2,1)} async-done(((bf16[256,2,16,256]{3,2,1,0:T(8,128)(2,1)}), bf16[256,2,16,256]{3,2,1,0:T(8,128)(2,1)}, u32[]{:S(2)}, u32[]{:S(2)}) %all-to-all-start.1) | async-done | bytes 4194336 | tf_op jit(solution)/shard_map/all_to_all | solution.py:262
  226.7 0.6 broadcast_in_dim.34.taps_ref
  227.3 16.0 %synthesis.1 = (bf16[8,1024,256]{2,1,0:T(8,128)(2,1)}, bf16[512,128]{1,0:T(8,128)(2,1)S(1)}) custom-call(bf16[1024,512]{1,0:T(8,128)(2,1)S(1)} %get-tuple-element.17.te_ref, bf16[1024,512]{1,0:T(8,128)(2,1)S(1)} %get-tuple-element.18.to_ref, f32[4,1024,128]{2,1,0:T(8,128)S(1)} %broadcast_in_dim.34.taps_ref, ...), custom_call_target="tpu_custom_call" | custom-call | tf_op jit(solution)/shard_map/synthesis/pallas_call | solution.py:195
  243.4 2.9 %collective-permute-start = (bf16[512,128]{1,0:T(8,128)(2,1)S(1)}, bf16[512,128]{1,0:T(8,128)(2,1)S(1)}, u32[]{:S(2)}, u32[]{:S(2)}) collective-permute-start(bf16[512,128]{1,0:T(8,128)(2,1)S(1)} %get-tuple-element.7), channel_id=1, source_target_pairs={{0,32},{32,64},{64,96},{96,128},{128,160},{160,192},{192,224},{1,3... | collective-permute-start | bytes 393224 | tf_op jit(solution)/shard_map/ppermute | solution.py:275
  246.3 5.2 %collective-permute-done.in_ref = bf16[512,128]{1,0:T(8,128)(2,1)S(1)} collective-permute-done((bf16[512,128]{1,0:T(8,128)(2,1)S(1)}, bf16[512,128]{1,0:T(8,128)(2,1)S(1)}, u32[]{:S(2)}, u32[]{:S(2)}) %collective-permute-start) | collective-permute-done | bytes 131104 | tf_op jit(solution)/shard_map/ppermute | solution.py:275
  251.5 7.4 %patch.1 = bf16[8,1024,256]{2,1,0:T(8,128)(2,1)} custom-call(bf16[512,128]{1,0:T(8,128)(2,1)S(1)} %collective-permute-done.in_ref, bf16[8,1024,256]{2,1,0:T(8,128)(2,1)} %get-tuple-element.8.series_ref), custom_call_target="tpu_custom_call", output_to_operand_aliasing={{}: (1, {})} | custom-call | tf_op jit(solution)/shard_map/patch/pallas_call | solution.py:239
  (8 shorter events, 0.1 us)
Async XLA Ops:
  0.0 3.4 %copy-start.4 = (bf16[16,1024,256]{2,1,0:T(8,128)(2,1)S(1)}, bf16[16,1024,256]{2,1,0:T(8,128)(2,1)}, u32[]{:S(2)}) copy-start(bf16[16,1024,256]{2,1,0:T(8,128)(2,1)} %volt_ref.1) | copy-start | bytes 25165828
  3.4 0.7 copy-start.5
  9.0 3.2 %copy-start.2 = (bf16[1024,16,256]{2,1,0:T(8,128)(2,1)}, bf16[1024,16,256]{2,1,0:T(8,128)(2,1)S(1)}, u32[]{:S(2)}) copy-start(bf16[1024,16,256]{2,1,0:T(8,128)(2,1)S(1)} %scale.1) | copy-start | bytes 25165828
  12.2 7.6 %copy-start.8 = (f32[512,32]{0,1:T(8,128)S(1)}, f32[512,32]{0,1:T(8,128)}, u32[]{:S(2)}) copy-start(f32[512,32]{0,1:T(8,128)} %param.8) | copy-start | bytes 196612
  12.2 7.7 %copy-start.9 = (f32[512,32]{0,1:T(8,128)S(1)}, f32[512,32]{0,1:T(8,128)}, u32[]{:S(2)}) copy-start(f32[512,32]{0,1:T(8,128)} %param.9) | copy-start | bytes 196612
  12.2 7.7 %copy-start.6 = (f32[512,256]{1,0:T(8,128)S(1)}, f32[512,256]{1,0:T(8,128)}, u32[]{:S(2)}) copy-start(f32[512,256]{1,0:T(8,128)} %param.10) | copy-start | bytes 1572868
  12.2 121.3 %all-to-all-start = ((bf16[1024,16,256]{2,1,0:T(8,128)(2,1)}), bf16[1024,16,256]{2,1,0:T(8,128)(2,1)}, u32[]{:S(2)}, u32[]{:S(2)}) async-start(bf16[1024,16,256]{2,1,0:T(8,128)(2,1)} %copy-done.2), calls=%async_computation | async-start | bytes 16777216 | tf_op jit(solution)/shard_map/all_to_all | solution.py:257
  133.5 3.4 %copy-start = (bf16[16,2,256,512]{3,2,1,0:T(8,128)(2,1)S(1)}, bf16[16,2,256,512]{3,2,1,0:T(8,128)(2,1)}, u32[]{:S(2)}) copy-start(bf16[16,2,256,512]{3,2,1,0:T(8,128)(2,1)} %get-tuple-element.9.wi_ref) | copy-start | bytes 25165828
  136.9 3.4 %copy-start.1 = (bf16[16,2,256,512]{3,2,1,0:T(8,128)(2,1)S(1)}, bf16[16,2,256,512]{3,2,1,0:T(8,128)(2,1)}, u32[]{:S(2)}) copy-start(bf16[16,2,256,512]{3,2,1,0:T(8,128)(2,1)} %get-tuple-element.10.wr_ref) | copy-start | bytes 25165828
  155.5 2.0 copy-start.3
  157.5 16.5 %copy-start.7 = (f32[4,1024]{1,0:T(4,128)S(1)}, f32[4,1024]{1,0:T(4,128)}, u32[]{:S(2)}) copy-start(f32[4,1024]{1,0:T(4,128)} %param.11) | copy-start | bytes 49156
  157.5 69.2 %all-to-all-start.1 = ((bf16[256,2,16,256]{3,2,1,0:T(8,128)(2,1)}), bf16[256,2,16,256]{3,2,1,0:T(8,128)(2,1)}, u32[]{:S(2)}, u32[]{:S(2)}) async-start(bf16[256,2,16,256]{3,2,1,0:T(8,128)(2,1)} %copy-done.3), calls=%async_computation.1 | async-start | bytes 8388608 | tf_op jit(solution)/shard_map/all_to_all | solution.py:262
  243.4 8.1 %collective-permute-start = (bf16[512,128]{1,0:T(8,128)(2,1)S(1)}, bf16[512,128]{1,0:T(8,128)(2,1)S(1)}, u32[]{:S(2)}, u32[]{:S(2)}) collective-permute-start(bf16[512,128]{1,0:T(8,128)(2,1)S(1)} %get-tuple-element.7), channel_id=1, source_target_pairs={{0,32},{32,64},{64,96},{96,128},{128,160},{160,192},{192,224},{1,3... | collective-permute-start | bytes 393224 | tf_op jit(solution)/shard_map/ppermute | solution.py:275

commit v2 on v1

v2 whole, which is shorter than its diff:
```python
import math

import jax
import jax.numpy as jnp
import ml_dtypes
import numpy as np
from jax import lax
from jax.experimental import pallas as pl
from jax.experimental.pallas import tpu as pltpu
from jax.sharding import PartitionSpec as P

C = 1024
TAPS = 4
TILE = 16
FR = 128
TWO_PI = 6.283185307179586
VMEM_MOST = 60 * 2**20


def swap_matrix():
    row = lax.broadcasted_iota(jnp.int32, (256, 256), 0)
    col = lax.broadcasted_iota(jnp.int32, (256, 256), 1)
    hit = (row // TILE == col % TILE) & (row % TILE == col // TILE)
    return jnp.where(hit, 1.0, 0.0).astype(jnp.bfloat16)


def parity_table(parity):
    sample = np.arange(C // 2)[:, None]
    channel = 2 * np.arange(C // 2)[None, :] + parity
    phases = TWO_PI / C * (sample * channel % C)
    both = np.concatenate([np.cos(phases), np.sin(phases)], axis=0) / math.sqrt(C)
    return both.astype(np.float32).astype(ml_dtypes.bfloat16)


def circle(turns):
    rest = turns - jnp.round(turns)
    half = math.pi * rest
    square = half * half
    sine = jnp.full_like(half, SIN_TERMS[-1])
    for term in SIN_TERMS[-2::-1]:
        sine = sine * square + term
    sine = sine * half
    cosine = jnp.full_like(half, COS_TERMS[-1])
    for term in COS_TERMS[-2::-1]:
        cosine = cosine * square + term
    return 1.0 - 2.0 * sine * sine, 2.0 * sine * cosine


SIN_TERMS = [(-1) ** i / math.factorial(2 * i + 1) for i in range(8)]
COS_TERMS = [(-1) ** i / math.factorial(2 * i) for i in range(8)]


SC_STEP = 128
CB = 64


def scale_kernel(exp_ref, volt_ref, out_ref, perm_ref):
    step = pl.program_id(0)

    @pl.when(step == 0)
    def _():
        perm_ref[...] = swap_matrix()

    station = lax.broadcasted_iota(jnp.int32, (TILE, 2 * FR), 0)
    for block in range(SC_STEP // CB):
        power = jnp.zeros((TILE, 2 * FR), jnp.int32)
        for s in range(TILE):
            power = jnp.where(station == s, exp_ref[s, step * (SC_STEP // CB) + block], power)
        factor = jnp.exp2(power.astype(jnp.float32)).astype(jnp.bfloat16).astype(jnp.float32)
        for part in range(CB // TILE):
            start = block * CB + part * TILE
            rows = volt_ref[:, start : start + TILE, :].reshape(256, 2 * FR)
            moved = jnp.dot(perm_ref[...], rows, preferred_element_type=jnp.float32)
            scaled = moved.reshape(TILE, TILE, 2 * FR) * factor[None]
            out_ref[start : start + TILE] = scaled.astype(jnp.bfloat16)


def scale_and_turn(voltages, exponents):
    return pl.pallas_call(
        scale_kernel,
        grid=(C // SC_STEP,),
        in_specs=[
            pl.BlockSpec(memory_space=pltpu.SMEM),
            pl.BlockSpec((TILE, SC_STEP, 2 * FR), lambda i: (0, i, 0)),
        ],
        out_specs=pl.BlockSpec((SC_STEP, TILE, 2 * FR), lambda i: (i, 0, 0)),
        out_shape=jax.ShapeDtypeStruct((C, TILE, 2 * FR), jnp.bfloat16),
        scratch_shapes=[pltpu.VMEM((256, 256), jnp.bfloat16)],
        compiler_params=pltpu.CompilerParams(vmem_limit_bytes=VMEM_MOST),
        name="scale",
    )(exponents, voltages)


CHUNK = 4
CHUNKS = 16 // CHUNK
BEAMS, STATIONS = 256, 512


def beam_kernel(
    start_ref,
    gr_ref,
    gi_ref,
    delay_ref,
    x_hbm,
    out_hbm,
    x_ref,
    out_ref,
    beams_ref,
    perm_ref,
    weight_a,
    weight_b,
    er_ref,
    ei_ref,
    sr_ref,
    si_ref,
    in_sems,
    out_sems,
):
    def arrival(q, j):
        part = pl.ds(j * CHUNK, CHUNK)
        return pltpu.make_async_copy(x_hbm.at[:, part, q], x_ref.at[q, :, part], in_sems.at[q, j])

    def departure(q):
        return pltpu.make_async_copy(out_ref.at[q], out_hbm.at[:, q], out_sems.at[q])

    for q in range(2):
        for j in range(CHUNKS):
            arrival(q, j).start()
    perm_ref[...] = swap_matrix()

    first = (start_ref[0].astype(jnp.float32) + 0.5) / C - 0.5
    for rows in range(0, BEAMS, 128):
        delay = jnp.transpose(delay_ref[:, rows : rows + 128])
        sr_ref[rows : rows + 128, :] = delay
    for rows in range(0, BEAMS, TILE):
        part = pl.ds(rows, TILE)
        delay = sr_ref[part, :]
        cosine, sine = circle(delay * first)
        er_ref[part, :] = cosine
        ei_ref[part, :] = -sine
        cosine, sine = circle(delay * (2.0 / C))
        sr_ref[part, :] = cosine
        si_ref[part, :] = -sine

    scale_factor = 1.0 / math.sqrt(STATIONS)

    def weigh(c, weight_ref):
        gr = gr_ref[pl.ds(c, 1), :] * scale_factor
        gi = gi_ref[pl.ds(c, 1), :] * scale_factor
        for rows in range(0, BEAMS, TILE):
            part = pl.ds(rows, TILE)
            er, ei = er_ref[part, :], ei_ref[part, :]
            weight_ref[part, :] = (gr * er - gi * ei).astype(jnp.bfloat16)
            weight_ref[pl.ds(BEAMS + rows, TILE), :] = (gi * er + gr * ei).astype(jnp.bfloat16)
            sr, si = sr_ref[part, :], si_ref[part, :]
            er_ref[part, :] = er * sr - ei * si
            ei_ref[part, :] = ei * sr + er * si

    def multiply(q, i, weight_ref):
        x = x_ref[q, :, i].reshape(STATIONS, 2 * FR)
        product = jnp.dot(weight_ref[...], x, preferred_element_type=jnp.float32)
        real = product[:BEAMS, :FR] - product[BEAMS:, FR:]
        imag = product[:BEAMS, FR:] + product[BEAMS:, :FR]
        beams_ref[i, :, :FR] = real.astype(jnp.bfloat16)
        beams_ref[i, :, FR:] = imag.astype(jnp.bfloat16)

    for q in range(2):
        if q == 1:
            for rows in range(0, BEAMS, 128):
                er_ref[rows : rows + 128, :] = jnp.transpose(delay_ref[:, rows : rows + 128])
            for rows in range(0, BEAMS, TILE):
                part = pl.ds(rows, TILE)
                cosine, sine = circle(er_ref[part, :] * (first + 1.0 / C))
                er_ref[part, :] = cosine
                ei_ref[part, :] = -sine

        def chunk(j, carry, q=q):
            arrival(q, j).wait()
            buffers = (weight_a, weight_b)
            for k in range(CHUNK):
                i = j * CHUNK + k
                weigh(2 * i + q, buffers[k % 2])
                multiply(q, i, buffers[k % 2])
            return carry

        lax.fori_loop(0, CHUNKS, chunk, 0)

        def turn(group, carry, q=q):
            part = pl.ds(pl.multiple_of(group * TILE, TILE), TILE)
            rows = beams_ref[:, part, :].reshape(256, 2 * FR)
            moved = jnp.dot(perm_ref[...], rows, preferred_element_type=jnp.float32)
            out_ref[q, part] = moved.reshape(TILE, TILE, 2 * FR).astype(jnp.bfloat16)
            return carry

        lax.fori_loop(0, BEAMS // TILE, turn, 0, unroll=4)
        departure(q).start()
    for q in range(2):
        departure(q).wait()


def form_beams(chan_start, gain_real, gain_imag, delays, received):
    whole = pl.BlockSpec(memory_space=pltpu.VMEM)
    remote = pl.BlockSpec(memory_space=pl.ANY)
    phasor = pltpu.VMEM((BEAMS, STATIONS), jnp.float32)
    weight = pltpu.VMEM((2 * BEAMS, STATIONS), jnp.bfloat16)
    return pl.pallas_call(
        beam_kernel,
        in_specs=[pl.BlockSpec(memory_space=pltpu.SMEM), whole, whole, whole, remote],
        out_specs=remote,
        out_shape=jax.ShapeDtypeStruct((BEAMS, 2, TILE, 2 * FR), jnp.bfloat16),
        scratch_shapes=[
            pltpu.VMEM((2, 32, 16, TILE, 2 * FR), jnp.bfloat16),
            pltpu.VMEM((2, BEAMS, TILE, 2 * FR), jnp.bfloat16),
            pltpu.VMEM((16, BEAMS, 2 * FR), jnp.bfloat16),
            pltpu.VMEM((256, 256), jnp.bfloat16),
            weight,
            weight,
            phasor,
            phasor,
            phasor,
            phasor,
            pltpu.SemaphoreType.DMA((2, CHUNKS)),
            pltpu.SemaphoreType.DMA((2,)),
        ],
        compiler_params=pltpu.CompilerParams(vmem_limit_bytes=58 * 2**20),
        name="beamform",
    )(chan_start, gain_real, gain_imag, delays, received.reshape(32, 16, 2, TILE, 2 * FR))


HALF = C // 2
ROWS = 64
LOCAL_BEAMS = 8


def transform(te_ref, to_ref, y_ref, beam, even_ref, odd_ref):
    even = y_ref[:, beam, 0].reshape(HALF, 2 * FR)
    odd = y_ref[:, beam, 1].reshape(HALF, 2 * FR)
    even_ref[...] = jnp.dot(te_ref[...], even, preferred_element_type=jnp.float32)
    odd_ref[...] = jnp.dot(to_ref[...], odd, preferred_element_type=jnp.float32)


def combine(taps_ref, beam, even_ref, odd_ref, pack_ref, out_ref):
    lane = lax.broadcasted_iota(jnp.int32, (ROWS, FR), 1)
    slot = lane // 4
    row = lax.rem(beam + LOCAL_BEAMS + 1, LOCAL_BEAMS + 1)
    for r in range(0, HALF, ROWS):
        cos_rows, sin_rows = pl.ds(r, ROWS), pl.ds(HALF + r, ROWS)
        parts = []
        for ref in (even_ref, odd_ref):
            real = ref[cos_rows, :FR] - ref[sin_rows, FR:]
            imag = ref[sin_rows, :FR] + ref[cos_rows, FR:]
            parts.append((real, imag))
        packed = pack_ref[cos_rows, :]
        for n1 in range(2):
            rows = pl.ds(n1 * HALF + r, ROWS)
            for ri in range(2):
                a, b = parts[0][ri], parts[1][ri]
                signal = a + b if n1 == 0 else a - b
                total = taps_ref[0, rows, :] * signal
                for k in range(1, TAPS):
                    shifted = jnp.where(lane >= k, pltpu.roll(signal, k, 1), 0.0)
                    total += taps_ref[k, rows, :] * shifted
                out_ref[row, rows, ri * FR : (ri + 1) * FR] = total.astype(jnp.bfloat16)
                where = beam * 4 + n1 * 2 + ri
                packed = jnp.where(
                    slot == where, pltpu.roll(signal, lax.rem(where * 4 + 4 + FR, FR), 1), packed
                )
        pack_ref[cos_rows, :] = packed


def synth_kernel(te_hbm, to_hbm, narrow_ref, y_ref, out_ref, tail_ref, *scratch):
    buffers, (pack_ref, te_ref, to_ref, taps_ref, sems) = (scratch[0:2], scratch[2:4]), scratch[4:]
    step = pl.program_id(0)
    last = pl.num_programs(0) - 1

    @pl.when(step == 0)
    def _():
        copies = [
            pltpu.make_async_copy(te_hbm, te_ref, sems.at[0]),
            pltpu.make_async_copy(to_hbm, to_ref, sems.at[1]),
        ]
        for copy in copies:
            copy.start()
        narrow = narrow_ref[...]
        columns = jnp.transpose(jnp.concatenate([narrow, narrow], axis=0))
        for k in range(TAPS):
            taps_ref[k] = jnp.broadcast_to(columns[:, k : k + 1], (C, FR))
        for copy in copies:
            copy.wait()

    def half(i):
        done = 2 * step + i - 1
        transform(te_ref, to_ref, y_ref, i, *buffers[i])
        combine(taps_ref, done, *buffers[1 - i], pack_ref, out_ref)

    half(0)

    @pl.when(step < last)
    def _():
        half(1)

    @pl.when(step == last)
    def _():
        lane = lax.broadcasted_iota(jnp.int32, (ROWS, FR), 1)
        for r in range(0, HALF, ROWS):
            rows = pl.ds(r, ROWS)
            packed = pack_ref[rows, :]
            total = jnp.zeros((ROWS, FR), jnp.float32)
            for k in range(1, TAPS):
                moved = jnp.where(lane % 4 < k, pltpu.roll(packed, FR - (4 - k), 1), 0.0)
                taps = jnp.where(
                    lane // 8 % 2 == 0, taps_ref[k, rows, :], taps_ref[k, pl.ds(HALF + r, ROWS), :]
                )
                total += taps * moved
            tail_ref[rows, :] = total.astype(jnp.bfloat16)


def synthesize(filter_taps, received):
    whole = pl.BlockSpec(memory_space=pltpu.VMEM)
    remote = pl.BlockSpec(memory_space=pl.ANY)
    steps = LOCAL_BEAMS // 2 + 1
    product = pltpu.VMEM((C, 2 * FR), jnp.float32)
    table = pltpu.VMEM((C, HALF), jnp.bfloat16)
    return pl.pallas_call(
        synth_kernel,
        grid=(steps,),
        in_specs=[
            remote,
            remote,
            whole,
            pl.BlockSpec(
                (32, 2, 2, TILE, 2 * FR), lambda g: (0, jnp.minimum(g, steps - 2), 0, 0, 0)
            ),
        ],
        out_specs=[whole, whole],
        out_shape=[
            jax.ShapeDtypeStruct((LOCAL_BEAMS + 1, C, 2 * FR), jnp.bfloat16),
            jax.ShapeDtypeStruct((HALF, FR), jnp.bfloat16),
        ],
        scratch_shapes=[product] * 4
        + [
            pltpu.VMEM((HALF, FR), jnp.float32),
            table,
            table,
            pltpu.VMEM((TAPS, C, FR), jnp.float32),
            pltpu.SemaphoreType.DMA((2,)),
        ],
        compiler_params=pltpu.CompilerParams(vmem_limit_bytes=40 * 2**20),
        name="synthesis",
    )(jnp.asarray(parity_table(0)), jnp.asarray(parity_table(1)), filter_taps, received)


def patch_kernel(in_ref, series_ref, out_ref):
    beam = pl.program_id(0)
    lane = lax.broadcasted_iota(jnp.int32, (FR, 2 * FR), 0)
    target = lax.broadcasted_iota(jnp.int32, (FR, 2 * FR), 1)
    frame, ri = target % FR, target // FR
    for n1 in range(2):
        slot = beam * 4 + n1 * 2 + ri
        spread = jnp.where((frame < TAPS - 1) & (lane == slot * 4 + frame), 1.0, 0.0)
        rows = pl.ds(n1 * HALF, HALF)
        head = jnp.dot(
            in_ref[...], spread.astype(jnp.bfloat16), preferred_element_type=jnp.float32
        )
        out_ref[0, rows, :] = (series_ref[beam, rows, :].astype(jnp.float32) + head).astype(
            jnp.bfloat16
        )


def patch(incoming, series):
    whole = pl.BlockSpec(memory_space=pltpu.VMEM)
    return pl.pallas_call(
        patch_kernel,
        grid=(LOCAL_BEAMS,),
        in_specs=[whole, whole],
        out_specs=pl.BlockSpec((1, C, 2 * FR), lambda b: (b, 0, 0)),
        out_shape=jax.ShapeDtypeStruct((LOCAL_BEAMS, C, 2 * FR), jnp.bfloat16),
        compiler_params=pltpu.CompilerParams(vmem_limit_bytes=16 * 2**20),
        name="patch",
    )(incoming, series)


def per_device(voltages, exponents, gain_real, gain_imag, delays, filter_taps):
    local_count = gain_real.shape[1]
    chan_start = (lax.axis_index("chan") * local_count).astype(jnp.int32).reshape(1)
    turned = scale_and_turn(voltages, exponents.reshape(TILE, -1))
    turned, chan_start = lax.optimization_barrier((turned, chan_start))
    received = lax.all_to_all(turned, "chan", split_axis=0, concat_axis=0, tiled=True)
    beamed = form_beams(
        chan_start, jnp.transpose(gain_real), jnp.transpose(gain_imag), delays, received
    )
    spectra = lax.all_to_all(beamed, "chan", split_axis=0, concat_axis=0, tiled=True)
    series, tail = synthesize(filter_taps, spectra.reshape(32, LOCAL_BEAMS, 2, TILE, 2 * FR))
    groups = lax.axis_size("tm")
    incoming = lax.ppermute(tail, "tm", [(g, g + 1) for g in range(groups - 1)])
    return patch(incoming, series)


def solution(mesh):
    placed = (
        P("chan", None, "tm"),
        P("chan", None, "tm"),
        P(None, "chan"),
        P(None, "chan"),
        P(),
        P(),
    )
    return jax.shard_map(
        per_device, mesh=mesh, in_specs=placed, out_specs=P("chan", None, "tm"), check_vma=False
    )
```

time: 262 us -> 213 us (0.81)
  blocking collectives: 0 us -> 158 us
  waiting for transfers between devices: 95.8 us -> 5.93 us
  other arithmetic: 75.5 us -> 0 us
  starting transfers between devices: 27 us -> 2.96 us
  local copies, waits for them, and re-layouts: 17 us -> 0.02 us
    all_to_all x0 -> x2, blocking collectives: none -> 158 us  [the longest x1 103 us: per_device(): lax.all_to_all(turned, 'chan', split_axis=0, concat_axis=0, tiled=True)]
    all_to_all x2 -> x0, waiting for transfers between devices: 90.6 us -> none  [the longest x1 47.5 us: per_device(): lax.all_to_all(turned, 'chan', split_axis=0, concat_axis=0, tiled=True)]
    convert_element_type x3 -> x0, other arithmetic: 74.8 us -> none  [the longest x1 65.9 us: beam_weights(): return (weight_real.astype(jnp.bfloat16), weight_imag.astype(jnp.bfloat16))]
    all_to_all x2 -> x0, starting transfers between devices: 24 us -> none  [the longest x1 16.5 us: per_device(): lax.all_to_all(beamed, 'chan', split_axis=0, concat_axis=0, tiled=True)]
    unnamed x20 -> x6, local copies, waits for them, and re-layouts: 16.1 us -> 0.02 us
    pallas_call x1, Pallas kernels: 4.88 us -> 10.5 us  [scale_and_turn(): pl.pallas_call(scale_kernel, grid=(C // SC_STEP,), in_specs=[pl.BlockSpec...]
    pallas_call x3, Pallas kernels: 38.6 us -> 35.3 us  [the longest x1 18.4 us: form_beams(): pl.pallas_call(beam_kernel, in_specs=[pl.BlockSpec(memory_space=pltpu.SME...]
  transfers between devices with their start and end apart: 3 -> 1, of which waited for: 3 -> 1; matrix products, arithmetic and copies ran while one was open for 29% -> 0% of each run, Pallas kernels for 0% -> 0%
where the time goes in v2:
time: 213 us; the launch traced here: 212 us
  blocking collectives  158 us (74%)
  Pallas kernels  45.9 us (22%)
  waiting for transfers between devices  5.93 us (3%)
  starting transfers between devices  2.96 us (1%)
    all_to_all x1, blocking collectives, per_device(): lax.all_to_all(turned, 'chan', split_axis=0, concat_axis=0, tiled=True)  103 us
    all_to_all x1, blocking collectives, per_device(): lax.all_to_all(beamed, 'chan', split_axis=0, concat_axis=0, tiled=True)  54.7 us
    pallas_call x1, Pallas kernels, form_beams(): pl.pallas_call(beam_kernel, in_specs=[pl.BlockSpec(memory_space=pltpu.SME...  18.4 us
    pallas_call x1, Pallas kernels, synthesize(): pl.pallas_call(synth_kernel, grid=(steps,), in_specs=[remote, remote, who...  12.2 us
    pallas_call x1, Pallas kernels, scale_and_turn(): pl.pallas_call(scale_kernel, grid=(C // SC_STEP,), in_specs=[pl.BlockSpec...  10.5 us
    ppermute x1, waiting for transfers between devices, per_device(): incoming = lax.ppermute(tail, 'tm', [(g, g + 1) for g in range(groups - 1)])  5.93 us
    pallas_call x1, Pallas kernels, patch(): pl.pallas_call(patch_kernel, grid=(LOCAL_BEAMS,), in_specs=[whole, whole]...  4.65 us
  transfers between devices with their start and end apart: 1, of which 1 were waited for; matrix products, arithmetic and copies ran while one was open for 0% of the time, Pallas kernels for 0%

profile of v2, /device:TPU:128, one launch (start us, length us, event | category | flops | bytes accessed | tf_op | source)
XLA Modules:
  0.0 212.4 jit_solution(1504382694521066883)
XLA Ops:
  0.0 10.5 %scale.1 = bf16[1024,16,256]{2,1,0:T(8,128)(2,1)} custom-call(s32[16,16]{1,0:T(8,128)} %bitcast.10, bf16[16,1024,256]{2,1,0:T(8,128)(2,1)} %volt_ref.1), custom_call_target="tpu_custom_call" | custom-call | tf_op jit(solution)/shard_map/scale/pallas_call | solution.py:79
  10.5 102.9 %all_to_all.10 = bf16[1024,16,256]{2,1,0:T(8,128)(2,1)} all-to-all(bf16[1024,16,256]{2,1,0:T(8,128)(2,1)} %scale.1), channel_id=1, replica_groups=mesh['tm'=8,'chan'=32] {'chan'}, dimensions={0} | all-to-all | bytes 16777216 | tf_op jit(solution)/shard_map/all_to_all | solution.py:388
  113.4 18.4 %beamform.1 = bf16[256,2,16,256]{3,2,1,0:T(8,128)(2,1)} custom-call(s32[1]{0:T(128)} %bitcast.1.start_ref, f32[32,512]{1,0:T(8,128)} %bitcast.8, f32[32,512]{1,0:T(8,128)} %bitcast.9, f32[512,256]{1,0:T(8,128)} %delay_ref.1, bf16[32,16,2,16,256]{4,3,2,1,0:T(8,128)(2,1)} %bitcast.7), custom_call_target="tpu_custom_call" | custom-call | tf_op jit(solution)/shard_map/beamform/pallas_call | solution.py:206
  131.9 0.0 copy-start
  131.9 0.0 copy-start.1
  131.9 0.0 copy-start.2
  131.9 54.7 %all_to_all.11 = bf16[256,2,16,256]{3,2,1,0:T(8,128)(2,1)S(1)} all-to-all(bf16[256,2,16,256]{3,2,1,0:T(8,128)(2,1)} %beamform.1), channel_id=1, replica_groups=mesh['tm'=8,'chan'=32] {'chan'}, dimensions={0} | all-to-all | bytes 8388608 | tf_op jit(solution)/shard_map/all_to_all | solution.py:392
  186.6 0.0 copy-done
  186.6 0.0 copy-done.1
  186.6 0.0 copy-done.2
  186.6 12.2 %synthesis.1 = (bf16[9,1024,256]{2,1,0:T(8,128)(2,1)S(1)}, bf16[512,128]{1,0:T(8,128)(2,1)S(1)}) custom-call(bf16[1024,512]{1,0:T(8,128)(2,1)S(1)} %copy-done.1, bf16[1024,512]{1,0:T(8,128)(2,1)S(1)} %copy-done, f32[4,1024]{1,0:T(4,128)S(1)} %copy-done.2, bf16[32,8,2,16,256]{4,3,2,1,0:T(8,128)(2,1)S(1)} %bitcast.6), custom_call_target="tpu_custom_call" | custom-call | tf_op jit(solution)/shard_map/synthesis/pallas_call | solution.py:324
  198.9 3.0 %collective-permute-start = (bf16[512,128]{1,0:T(8,128)(2,1)S(1)}, bf16[512,128]{1,0:T(8,128)(2,1)S(1)}, u32[]{:S(2)}, u32[]{:S(2)}) collective-permute-start(bf16[512,128]{1,0:T(8,128)(2,1)S(1)} %get-tuple-element.11), channel_id=1, source_target_pairs={{0,32},{32,64},{64,96},{96,128},{128,160},{160,192},{192,224},{1,3... | collective-permute-start | bytes 393224 | tf_op jit(solution)/shard_map/ppermute | solution.py:395
  201.8 5.9 %collective-permute-done.in_ref = bf16[512,128]{1,0:T(8,128)(2,1)S(1)} collective-permute-done((bf16[512,128]{1,0:T(8,128)(2,1)S(1)}, bf16[512,128]{1,0:T(8,128)(2,1)S(1)}, u32[]{:S(2)}, u32[]{:S(2)}) %collective-permute-start) | collective-permute-done | bytes 131104 | tf_op jit(solution)/shard_map/ppermute | solution.py:395
  207.8 4.6 %patch.1 = bf16[8,1024,256]{2,1,0:T(8,128)(2,1)} custom-call(bf16[512,128]{1,0:T(8,128)(2,1)S(1)} %collective-permute-done.in_ref, bf16[9,1024,256]{2,1,0:T(8,128)(2,1)S(1)} %get-tuple-element.12.series_ref), custom_call_target="tpu_custom_call" | custom-call | tf_op jit(solution)/shard_map/patch/pallas_call | solution.py:372
Async XLA Ops:
  131.9 54.8 %copy-start = (bf16[1024,512]{1,0:T(8,128)(2,1)S(1)}, bf16[1024,512]{1,0:T(8,128)(2,1)}, u32[]{:S(2)}) copy-start(bf16[1024,512]{1,0:T(8,128)(2,1)} %constant.11.clone.to_hbm) | copy-start | bytes 3145732
  131.9 54.8 %copy-start.1 = (bf16[1024,512]{1,0:T(8,128)(2,1)S(1)}, bf16[1024,512]{1,0:T(8,128)(2,1)}, u32[]{:S(2)}) copy-start(bf16[1024,512]{1,0:T(8,128)(2,1)} %constant.10.clone.te_hbm) | copy-start | bytes 3145732
  131.9 54.7 %copy-start.2 = (f32[4,1024]{1,0:T(4,128)S(1)}, f32[4,1024]{1,0:T(4,128)}, u32[]{:S(2)}) copy-start(f32[4,1024]{1,0:T(4,128)} %narrow_ref.1) | copy-start | bytes 49156
  198.9 8.9 %collective-permute-start = (bf16[512,128]{1,0:T(8,128)(2,1)S(1)}, bf16[512,128]{1,0:T(8,128)(2,1)S(1)}, u32[]{:S(2)}, u32[]{:S(2)}) collective-permute-start(bf16[512,128]{1,0:T(8,128)(2,1)S(1)} %get-tuple-element.11), channel_id=1, source_target_pairs={{0,32},{32,64},{64,96},{96,128},{128,160},{160,192},{192,224},{1,3... | collective-permute-start | bytes 393224 | tf_op jit(solution)/shard_map/ppermute | solution.py:395

commit v3 on v2

v3 whole, which is shorter than its diff:
```python
import math

import jax
import jax.numpy as jnp
import ml_dtypes
import numpy as np
from jax import lax
from jax.experimental import pallas as pl
from jax.experimental.pallas import tpu as pltpu
from jax.sharding import PartitionSpec as P

C = 1024
TAPS = 4
TILE = 16
FR = 128
TWO_PI = 6.283185307179586
VMEM_MOST = 60 * 2**20
SYNTH_VMEM = 32 * 2**20
BEAM_VMEM = 36 * 2**20


def swap_matrix():
    row = lax.broadcasted_iota(jnp.int32, (256, 256), 0)
    col = lax.broadcasted_iota(jnp.int32, (256, 256), 1)
    hit = (row // TILE == col % TILE) & (row % TILE == col // TILE)
    return jnp.where(hit, 1.0, 0.0).astype(jnp.bfloat16)


def parity_table(parity):
    sample = np.arange(C // 2)[:, None]
    channel = 2 * np.arange(C // 2)[None, :] + parity
    phases = TWO_PI / C * (sample * channel % C)
    both = np.concatenate([np.cos(phases), np.sin(phases)], axis=0) / math.sqrt(C)
    return both.astype(np.float32).astype(ml_dtypes.bfloat16)


def circle(turns):
    rest = turns - jnp.round(turns)
    half = math.pi * rest
    square = half * half
    sine = jnp.full_like(half, SIN_TERMS[-1])
    for term in SIN_TERMS[-2::-1]:
        sine = sine * square + term
    sine = sine * half
    cosine = jnp.full_like(half, COS_TERMS[-1])
    for term in COS_TERMS[-2::-1]:
        cosine = cosine * square + term
    return 1.0 - 2.0 * sine * sine, 2.0 * sine * cosine


SIN_TERMS = [(-1) ** i / math.factorial(2 * i + 1) for i in range(7)]
COS_TERMS = [(-1) ** i / math.factorial(2 * i) for i in range(7)]


SC_STEP = 128
CB = 64


def scale_kernel(exp_ref, volt_hbm, out_hbm, volt_ref, out_ref, perm_ref, in_sems, out_sems):
    def arrival(j):
        part = pl.ds(j * SC_STEP, SC_STEP)
        return pltpu.make_async_copy(volt_hbm.at[:, part], volt_ref.at[:, part], in_sems.at[j])

    def departure(j):
        part = pl.ds(j * SC_STEP, SC_STEP)
        return pltpu.make_async_copy(out_ref.at[part], out_hbm.at[part], out_sems.at[j])

    steps = C // SC_STEP
    for j in range(steps):
        arrival(j).start()
    perm_ref[...] = swap_matrix()
    station = lax.broadcasted_iota(jnp.int32, (TILE, 2 * FR), 0)

    def scale(j, carry):
        arrival(j).wait()
        for block in range(SC_STEP // CB):
            power = jnp.zeros((TILE, 2 * FR), jnp.int32)
            for s in range(TILE):
                power = jnp.where(station == s, exp_ref[s, j * (SC_STEP // CB) + block], power)
            factor = jnp.exp2(power.astype(jnp.float32)).astype(jnp.bfloat16).astype(jnp.float32)
            for part in range(CB // TILE):
                start = pl.multiple_of(j * SC_STEP + block * CB + part * TILE, TILE)
                rows = volt_ref[:, pl.ds(start, TILE), :].reshape(256, 2 * FR)
                moved = jnp.dot(perm_ref[...], rows, preferred_element_type=jnp.float32)
                scaled = moved.reshape(TILE, TILE, 2 * FR) * factor[None]
                out_ref[pl.ds(start, TILE)] = scaled.astype(jnp.bfloat16)
        departure(j).start()
        return carry

    lax.fori_loop(0, steps, scale, 0)
    for j in range(steps):
        departure(j).wait()


def scale_and_turn(voltages, exponents):
    remote = pl.BlockSpec(memory_space=pl.ANY)
    return pl.pallas_call(
        scale_kernel,
        in_specs=[pl.BlockSpec(memory_space=pltpu.SMEM), remote],
        out_specs=remote,
        out_shape=jax.ShapeDtypeStruct((C, TILE, 2 * FR), jnp.bfloat16),
        scratch_shapes=[
            pltpu.VMEM((TILE, C, 2 * FR), jnp.bfloat16),
            pltpu.VMEM((C, TILE, 2 * FR), jnp.bfloat16),
            pltpu.VMEM((256, 256), jnp.bfloat16),
            pltpu.SemaphoreType.DMA((C // SC_STEP,)),
            pltpu.SemaphoreType.DMA((C // SC_STEP,)),
        ],
        compiler_params=pltpu.CompilerParams(vmem_limit_bytes=VMEM_MOST),
        name="scale",
    )(exponents, voltages)


CHUNK = 4
CHUNKS = 16 // CHUNK
BEAMS, STATIONS = 256, 512


def beam_kernel(
    start_ref,
    gr_ref,
    gi_ref,
    delay_ref,
    x_ref,
    out_hbm,
    out_ref,
    beams_even,
    beams_odd,
    perm_ref,
    weight_a,
    weight_b,
    er_ref,
    ei_ref,
    pr_ref,
    pi_ref,
    two_ref,
    gain_ref,
    out_sems,
):
    def departure(q):
        return pltpu.make_async_copy(out_ref.at[q], out_hbm.at[:, q], out_sems.at[q])

    beams_refs = (beams_even, beams_odd)
    perm_ref[...] = swap_matrix()

    first = (start_ref[0].astype(jnp.float32) + 0.5) / C - 0.5
    for rows in range(0, BEAMS, 128):
        two_ref[rows : rows + 128, :] = jnp.transpose(delay_ref[:, rows : rows + 128])
    for rows in range(0, BEAMS, TILE):
        part = pl.ds(rows, TILE)
        delay = two_ref[part, :]
        ar, sine = circle(delay * first)
        ai = -sine
        angle = delay * (TWO_PI / C)
        square = angle * angle
        c1 = 1.0 + square * (-1.0 / 2 + square * (1.0 / 24))
        s1 = angle * (1.0 + square * (-1.0 / 6 + square * (1.0 / 120)))
        c2, s2 = 1.0 - 2.0 * s1 * s1, 2.0 * s1 * c1
        two_ref[part, :] = 2.0 * c2
        er_ref[0, part, :], ei_ref[0, part, :] = ar, ai
        pr_ref[0, part, :], pi_ref[0, part, :] = ar * c2 - ai * s2, ai * c2 + ar * s2
        rc, rs, ic, is_ = ar * c1, ar * s1, ai * c1, ai * s1
        er_ref[1, part, :], ei_ref[1, part, :] = rc + is_, ic - rs
        pr_ref[1, part, :], pi_ref[1, part, :] = rc - is_, ic + rs

    scale_factor = 1.0 / math.sqrt(STATIONS)
    for part, ref in enumerate((gr_ref, gi_ref)):
        for c in range(ref.shape[0]):
            gain_ref[part, c] = ref[c : c + 1, :] * scale_factor

    def weigh(q, j, weight_ref, block):
        lanes = slice(block * 128, (block + 1) * 128)
        gains = []
        for k in range(CHUNK):
            c = 2 * (j * CHUNK + k) + q
            gains.append((gain_ref[0, c, :, lanes], gain_ref[1, c, :, lanes]))
        for rows in range(0, BEAMS, TILE):
            part, below = pl.ds(rows, TILE), pl.ds(BEAMS + rows, TILE)
            er, ei = er_ref[q, part, lanes], ei_ref[q, part, lanes]
            pr, pi = pr_ref[q, part, lanes], pi_ref[q, part, lanes]
            two = two_ref[part, lanes]
            for k, (gr, gi) in enumerate(gains):
                weight_ref[k, part, lanes] = (gr * er - gi * ei).astype(jnp.bfloat16)
                weight_ref[k, below, lanes] = (gi * er + gr * ei).astype(jnp.bfloat16)
                pr, er = er, two * er - pr
                pi, ei = ei, two * ei - pi
            er_ref[q, part, lanes], ei_ref[q, part, lanes] = er, ei
            pr_ref[q, part, lanes], pi_ref[q, part, lanes] = pr, pi

    def multiply(q, j, k, weight_ref):
        i = j * CHUNK + k
        x = x_ref[:, i, q].reshape(STATIONS, 2 * FR)
        product = jnp.dot(weight_ref[k], x, preferred_element_type=jnp.float32)
        real = product[:BEAMS, :FR] - product[BEAMS:, FR:]
        imag = product[:BEAMS, FR:] + product[BEAMS:, :FR]
        beams_refs[q][i, :, :FR] = real.astype(jnp.bfloat16)
        beams_refs[q][i, :, FR:] = imag.astype(jnp.bfloat16)

    def turn(q, group):
        part = pl.ds(pl.multiple_of(group * TILE, TILE), TILE)
        rows = beams_refs[q][:, part, :].reshape(256, 2 * FR)
        moved = jnp.dot(perm_ref[...], rows, preferred_element_type=jnp.float32)
        out_ref[q, part] = moved.reshape(TILE, TILE, 2 * FR).astype(jnp.bfloat16)

    groups = BEAMS // TILE
    for block in range(STATIONS // 128):
        weigh(0, 0, weight_a, block)
    for q in range(2):

        def pair(m, carry, q=q):
            for h, (now, later) in enumerate(((weight_a, weight_b), (weight_b, weight_a))):
                n = q * CHUNKS + 2 * m + h
                following = jnp.minimum(n + 1, 2 * CHUNKS - 1)
                for k in range(CHUNK):
                    multiply(q, 2 * m + h, k, now)
                    weigh(following // CHUNKS, following % CHUNKS, later, k)
                    if q == 1:
                        turn(0, 4 * (2 * m + h) + k)
            return carry

        lax.fori_loop(0, CHUNKS // 2, pair, 0)
        if q == 1:
            departure(0).start()
    for group in range(groups):
        turn(1, group)
    departure(1).start()
    for q in range(2):
        departure(q).wait()


def form_beams(chan_start, gain_real, gain_imag, delays, received):
    whole = pl.BlockSpec(memory_space=pltpu.VMEM)
    phasor = pltpu.VMEM((2, BEAMS, STATIONS), jnp.float32)
    weight = pltpu.VMEM((CHUNK, 2 * BEAMS, STATIONS), jnp.bfloat16)
    return pl.pallas_call(
        beam_kernel,
        in_specs=[pl.BlockSpec(memory_space=pltpu.SMEM), whole, whole, whole, whole],
        out_specs=pl.BlockSpec(memory_space=pl.ANY),
        out_shape=jax.ShapeDtypeStruct((BEAMS, 2, TILE, 2 * FR), jnp.bfloat16),
        scratch_shapes=[
            pltpu.VMEM((2, BEAMS, TILE, 2 * FR), jnp.bfloat16),
            pltpu.VMEM((16, BEAMS, 2 * FR), jnp.bfloat16),
            pltpu.VMEM((16, BEAMS, 2 * FR), jnp.bfloat16),
            pltpu.VMEM((256, 256), jnp.bfloat16),
            weight,
            weight,
            phasor,
            phasor,
            phasor,
            phasor,
            pltpu.VMEM((BEAMS, STATIONS), jnp.float32),
            pltpu.VMEM((2, gain_real.shape[0], 1, STATIONS), jnp.float32),
            pltpu.SemaphoreType.DMA((2,)),
        ],
        compiler_params=pltpu.CompilerParams(vmem_limit_bytes=BEAM_VMEM),
        name="beamform",
    )(chan_start, gain_real, gain_imag, delays, received.reshape(32, 16, 2, TILE, 2 * FR))


HALF = C // 2
ROWS = 64
LOCAL_BEAMS = 8


def transform(te_ref, to_ref, y_ref, beam, even_ref, odd_ref):
    even = y_ref[:, beam, 0].reshape(HALF, 2 * FR)
    odd = y_ref[:, beam, 1].reshape(HALF, 2 * FR)
    even_ref[...] = jnp.dot(te_ref[...], even, preferred_element_type=jnp.float32)
    odd_ref[...] = jnp.dot(to_ref[...], odd, preferred_element_type=jnp.float32)


def combine(taps_ref, beam, even_ref, odd_ref, pack_ref, out_ref):
    lane = lax.broadcasted_iota(jnp.int32, (ROWS, FR), 1)
    slot = lane // 4
    row = lax.rem(beam + LOCAL_BEAMS + 1, LOCAL_BEAMS + 1)
    for r in range(0, HALF, ROWS):
        cos_rows, sin_rows = pl.ds(r, ROWS), pl.ds(HALF + r, ROWS)
        parts = []
        for ref in (even_ref, odd_ref):
            real = ref[cos_rows, :FR] - ref[sin_rows, FR:]
            imag = ref[sin_rows, :FR] + ref[cos_rows, FR:]
            parts.append((real, imag))
        packed = pack_ref[cos_rows, :]
        for n1 in range(2):
            rows = pl.ds(n1 * HALF + r, ROWS)
            for ri in range(2):
                a, b = parts[0][ri], parts[1][ri]
                signal = a + b if n1 == 0 else a - b
                total = taps_ref[0, rows, :] * signal
                for k in range(1, TAPS):
                    shifted = jnp.where(lane >= k, pltpu.roll(signal, k, 1), 0.0)
                    total += taps_ref[k, rows, :] * shifted
                out_ref[row, rows, ri * FR : (ri + 1) * FR] = total.astype(jnp.bfloat16)
                where = beam * 4 + n1 * 2 + ri
                packed = jnp.where(
                    slot == where, pltpu.roll(signal, lax.rem(where * 4 + 4 + FR, FR), 1), packed
                )
        pack_ref[cos_rows, :] = packed


def synth_kernel(te_ref, to_ref, narrow_ref, y_ref, out_ref, tail_ref, *scratch):
    buffers, (pack_ref, taps_ref) = (scratch[0:2], scratch[2:4]), scratch[4:]
    step = pl.program_id(0)

    @pl.when(step == 0)
    def _():
        narrow = narrow_ref[...]
        columns = jnp.transpose(jnp.concatenate([narrow, narrow], axis=0))
        for k in range(TAPS):
            taps_ref[k] = jnp.broadcast_to(columns[:, k : k + 1], (C, FR))

    last = pl.num_programs(0) - 1

    def half(i):
        done = 2 * step + i - 1
        arriving = jnp.minimum(2 * step + i, LOCAL_BEAMS - 1)
        transform(te_ref, to_ref, y_ref, arriving, *buffers[i])
        combine(taps_ref, done, *buffers[1 - i], pack_ref, out_ref)

    half(0)

    @pl.when(step < last)
    def _():
        half(1)

    @pl.when(step == last)
    def _():
        lane = lax.broadcasted_iota(jnp.int32, (ROWS, FR), 1)
        for r in range(0, HALF, ROWS):
            rows = pl.ds(r, ROWS)
            packed = pack_ref[rows, :]
            total = jnp.zeros((ROWS, FR), jnp.float32)
            for k in range(1, TAPS):
                moved = jnp.where(lane % 4 < k, pltpu.roll(packed, FR - (4 - k), 1), 0.0)
                taps = jnp.where(
                    lane // 8 % 2 == 0, taps_ref[k, rows, :], taps_ref[k, pl.ds(HALF + r, ROWS), :]
                )
                total += taps * moved
            tail_ref[rows, :] = total.astype(jnp.bfloat16)


def synthesize(filter_taps, received):
    whole = pl.BlockSpec(memory_space=pltpu.VMEM)
    steps = LOCAL_BEAMS // 2 + 1
    product = pltpu.VMEM((C, 2 * FR), jnp.float32)
    return pl.pallas_call(
        synth_kernel,
        grid=(steps,),
        in_specs=[whole] * 4,
        out_specs=[whole, whole],
        out_shape=[
            jax.ShapeDtypeStruct((LOCAL_BEAMS + 1, C, 2 * FR), jnp.bfloat16),
            jax.ShapeDtypeStruct((HALF, FR), jnp.bfloat16),
        ],
        scratch_shapes=[product] * 4
        + [pltpu.VMEM((HALF, FR), jnp.float32), pltpu.VMEM((TAPS, C, FR), jnp.float32)],
        compiler_params=pltpu.CompilerParams(vmem_limit_bytes=SYNTH_VMEM),
        name="synthesis",
    )(jnp.asarray(parity_table(0)), jnp.asarray(parity_table(1)), filter_taps, received)


PATCH_BEAMS = 4


def patch_kernel(in_ref, series_ref, out_ref):
    lane = lax.broadcasted_iota(jnp.int32, (FR, 2 * FR), 0)
    target = lax.broadcasted_iota(jnp.int32, (FR, 2 * FR), 1)
    frame, ri = target % FR, target // FR
    for i in range(PATCH_BEAMS):
        beam = pl.program_id(0) * PATCH_BEAMS + i
        for n1 in range(2):
            slot = beam * 4 + n1 * 2 + ri
            spread = jnp.where((frame < TAPS - 1) & (lane == slot * 4 + frame), 1.0, 0.0)
            rows = pl.ds(n1 * HALF, HALF)
            head = jnp.dot(
                in_ref[...], spread.astype(jnp.bfloat16), preferred_element_type=jnp.float32
            )
            out_ref[i, rows, :] = (series_ref[beam, rows, :].astype(jnp.float32) + head).astype(
                jnp.bfloat16
            )


def patch(incoming, series):
    whole = pl.BlockSpec(memory_space=pltpu.VMEM)
    return pl.pallas_call(
        patch_kernel,
        grid=(LOCAL_BEAMS // PATCH_BEAMS,),
        in_specs=[whole, whole],
        out_specs=pl.BlockSpec((PATCH_BEAMS, C, 2 * FR), lambda b: (b, 0, 0)),
        out_shape=jax.ShapeDtypeStruct((LOCAL_BEAMS, C, 2 * FR), jnp.bfloat16),
        compiler_params=pltpu.CompilerParams(vmem_limit_bytes=16 * 2**20),
        name="patch",
    )(incoming, series)


def per_device(voltages, exponents, gain_real, gain_imag, delays, filter_taps):
    local_count = gain_real.shape[1]
    chan_start = (lax.axis_index("chan") * local_count).astype(jnp.int32).reshape(1)
    turned = scale_and_turn(voltages, exponents.reshape(TILE, -1))
    turned, chan_start = lax.optimization_barrier((turned, chan_start))
    received = lax.all_to_all(turned, "chan", split_axis=0, concat_axis=0, tiled=True)
    beamed = form_beams(
        chan_start, jnp.transpose(gain_real), jnp.transpose(gain_imag), delays, received
    )
    spectra = lax.all_to_all(beamed, "chan", split_axis=0, concat_axis=0, tiled=True)
    series, tail = synthesize(filter_taps, spectra.reshape(32, LOCAL_BEAMS, 2, TILE, 2 * FR))
    groups = lax.axis_size("tm")
    incoming = lax.ppermute(tail, "tm", [(g, g + 1) for g in range(groups - 1)])
    return patch(incoming, series)


def solution(mesh):
    placed = (
        P("chan", None, "tm"),
        P("chan", None, "tm"),
        P(None, "chan"),
        P(None, "chan"),
        P(),
        P(),
    )
    return jax.shard_map(
        per_device, mesh=mesh, in_specs=placed, out_specs=P("chan", None, "tm"), check_vma=False
    )
```

time: 213 us -> 204 us (0.958)
  Pallas kernels: 45.9 us -> 37.6 us
    pallas_call x3, Pallas kernels: 27.4 us -> 22.3 us  [the longest x1 11.8 us: synthesize(): pl.pallas_call(synth_kernel, grid=(steps,), in_specs=[whole] * 4, out_spe...]
    pallas_call x1, Pallas kernels: 18.4 us -> 15.3 us  [form_beams(): pl.pallas_call(beam_kernel, in_specs=[pl.BlockSpec(memory_space=pltpu.SME...]
where the time goes in v3:
time: 204 us
  blocking collectives  157 us (77%)
  Pallas kernels  37.6 us (18%)
  waiting for transfers between devices  5.93 us (3%)
  starting transfers between devices  2.94 us (1%)
    all_to_all x1, blocking collectives, per_device(): lax.all_to_all(turned, 'chan', split_axis=0, concat_axis=0, tiled=True)  103 us
    all_to_all x1, blocking collectives, per_device(): lax.all_to_all(beamed, 'chan', split_axis=0, concat_axis=0, tiled=True)  54.5 us
    pallas_call x1, Pallas kernels, form_beams(): pl.pallas_call(beam_kernel, in_specs=[pl.BlockSpec(memory_space=pltpu.SME...  15.3 us
    pallas_call x1, Pallas kernels, synthesize(): pl.pallas_call(synth_kernel, grid=(steps,), in_specs=[whole] * 4, out_spe...  11.8 us
    pallas_call x1, Pallas kernels, scale_and_turn(): pl.pallas_call(scale_kernel, in_specs=[pl.BlockSpec(memory_space=pltpu.SM...  7.71 us
    ppermute x1, waiting for transfers between devices, per_device(): incoming = lax.ppermute(tail, 'tm', [(g, g + 1) for g in range(groups - 1)])  5.93 us
  transfers between devices with their start and end apart: 1, of which 1 were waited for; matrix products, arithmetic and copies ran while one was open for 0% of the time, Pallas kernels for 0%

profile of v3, /device:TPU:128, one launch (start us, length us, event | category | flops | bytes accessed | tf_op | source)
XLA Modules:
  0.0 204.0 jit_solution(10012207869787136726)
XLA Ops:
  0.0 7.7 %scale.1 = bf16[1024,16,256]{2,1,0:T(8,128)(2,1)} custom-call(s32[16,16]{1,0:T(8,128)} %bitcast.10, bf16[16,1024,256]{2,1,0:T(8,128)(2,1)} %volt_hbm.1), custom_call_target="tpu_custom_call" | custom-call | tf_op jit(solution)/shard_map/scale/pallas_call | solution.py:97
  7.7 0.0 copy-start.2
  7.7 0.0 copy-start.3
  7.7 0.0 copy-start.4
  7.8 102.9 %all_to_all.10 = bf16[1024,16,256]{2,1,0:T(8,128)(2,1)S(1)} all-to-all(bf16[1024,16,256]{2,1,0:T(8,128)(2,1)} %scale.1), channel_id=1, replica_groups=mesh['tm'=8,'chan'=32] {'chan'}, dimensions={0} | all-to-all | bytes 16777216 | tf_op jit(solution)/shard_map/all_to_all | solution.py:401
  110.7 0.0 copy-done.2
  110.7 0.0 copy-done.3
  110.7 0.0 copy-done.4
  110.7 15.3 %beamform.1 = bf16[256,2,16,256]{3,2,1,0:T(8,128)(2,1)S(1)} custom-call(s32[1]{0:T(128)} %bitcast.1.start_ref, f32[32,512]{1,0:T(8,128)S(1)} %bitcast.8, f32[32,512]{1,0:T(8,128)S(1)} %bitcast.9, f32[512,256]{1,0:T(8,128)S(1)} %copy-done.2, bf16[32,16,2,16,256]{4,3,2,1,0:T(8,128)(2,1)S(1)} %bitcast.6), custom_call_target="tpu_custom_call" | custom-call | tf_op jit(solution)/shard_map/beamform/pallas_call | solution.py:235
  126.0 0.0 copy-start
  126.1 0.0 copy-start.1
  126.1 0.0 copy-start.5
  126.1 54.5 %all_to_all.11 = bf16[256,2,16,256]{3,2,1,0:T(8,128)(2,1)S(1)} all-to-all(bf16[256,2,16,256]{3,2,1,0:T(8,128)(2,1)S(1)} %beamform.1), channel_id=1, replica_groups=mesh['tm'=8,'chan'=32] {'chan'}, dimensions={0} | all-to-all | bytes 8388608 | tf_op jit(solution)/shard_map/all_to_all | solution.py:405
  180.6 0.0 copy-done
  180.6 0.0 copy-done.1
  180.6 0.0 copy-done.5
  180.6 11.8 %synthesis.1 = (bf16[9,1024,256]{2,1,0:T(8,128)(2,1)S(1)}, bf16[512,128]{1,0:T(8,128)(2,1)S(1)}) custom-call(bf16[1024,512]{1,0:T(8,128)(2,1)S(1)} %copy-done.1, bf16[1024,512]{1,0:T(8,128)(2,1)S(1)} %copy-done, f32[4,1024]{1,0:T(4,128)S(1)} %copy-done.5, bf16[32,8,2,16,256]{4,3,2,1,0:T(8,128)(2,1)S(1)} %bitcast.7), custom_call_target="tpu_custom_call" | custom-call | tf_op jit(solution)/shard_map/synthesis/pallas_call | solution.py:346
  192.4 2.9 %collective-permute-start = (bf16[512,128]{1,0:T(8,128)(2,1)S(1)}, bf16[512,128]{1,0:T(8,128)(2,1)S(1)}, u32[]{:S(2)}, u32[]{:S(2)}) collective-permute-start(bf16[512,128]{1,0:T(8,128)(2,1)S(1)} %get-tuple-element.11), channel_id=1, source_target_pairs={{0,32},{32,64},{64,96},{96,128},{128,160},{160,192},{192,224},{1,3... | collective-permute-start | bytes 393224 | tf_op jit(solution)/shard_map/ppermute | solution.py:408
  195.3 5.9 %collective-permute-done.in_ref = bf16[512,128]{1,0:T(8,128)(2,1)S(1)} collective-permute-done((bf16[512,128]{1,0:T(8,128)(2,1)S(1)}, bf16[512,128]{1,0:T(8,128)(2,1)S(1)}, u32[]{:S(2)}, u32[]{:S(2)}) %collective-permute-start) | collective-permute-done | bytes 131104 | tf_op jit(solution)/shard_map/ppermute | solution.py:408
  201.3 2.8 %patch.1 = bf16[8,1024,256]{2,1,0:T(8,128)(2,1)} custom-call(bf16[512,128]{1,0:T(8,128)(2,1)S(1)} %collective-permute-done.in_ref, bf16[9,1024,256]{2,1,0:T(8,128)(2,1)S(1)} %get-tuple-element.12.series_ref), custom_call_target="tpu_custom_call" | custom-call | tf_op jit(solution)/shard_map/patch/pallas_call | solution.py:385
Async XLA Ops:
  7.7 103.0 %copy-start.2 = (f32[512,256]{1,0:T(8,128)S(1)}, f32[512,256]{1,0:T(8,128)}, u32[]{:S(2)}) copy-start(f32[512,256]{1,0:T(8,128)} %delay_ref.1) | copy-start | bytes 1572868
  7.7 103.0 %copy-start.3 = (f32[512,32]{0,1:T(8,128)S(1)}, f32[512,32]{0,1:T(8,128)}, u32[]{:S(2)}) copy-start(f32[512,32]{0,1:T(8,128)} %param.10) | copy-start | bytes 196612
  7.7 102.9 %copy-start.4 = (f32[512,32]{0,1:T(8,128)S(1)}, f32[512,32]{0,1:T(8,128)}, u32[]{:S(2)}) copy-start(f32[512,32]{0,1:T(8,128)} %param.11) | copy-start | bytes 196612
  126.0 54.5 %copy-start = (bf16[1024,512]{1,0:T(8,128)(2,1)S(1)}, bf16[1024,512]{1,0:T(8,128)(2,1)}, u32[]{:S(2)}) copy-start(bf16[1024,512]{1,0:T(8,128)(2,1)} %constant.11.clone.to_ref) | copy-start | bytes 3145732
  126.1 54.5 %copy-start.1 = (bf16[1024,512]{1,0:T(8,128)(2,1)S(1)}, bf16[1024,512]{1,0:T(8,128)(2,1)}, u32[]{:S(2)}) copy-start(bf16[1024,512]{1,0:T(8,128)(2,1)} %constant.10.clone.te_ref) | copy-start | bytes 3145732
  126.1 54.5 %copy-start.5 = (f32[4,1024]{1,0:T(4,128)S(1)}, f32[4,1024]{1,0:T(4,128)}, u32[]{:S(2)}) copy-start(f32[4,1024]{1,0:T(4,128)} %narrow_ref.1) | copy-start | bytes 49156
  192.4 8.9 %collective-permute-start = (bf16[512,128]{1,0:T(8,128)(2,1)S(1)}, bf16[512,128]{1,0:T(8,128)(2,1)S(1)}, u32[]{:S(2)}, u32[]{:S(2)}) collective-permute-start(bf16[512,128]{1,0:T(8,128)(2,1)S(1)} %get-tuple-element.11), channel_id=1, source_target_pairs={{0,32},{32,64},{64,96},{96,128},{128,160},{160,192},{192,224},{1,3... | collective-permute-start | bytes 393224 | tf_op jit(solution)/shard_map/ppermute | solution.py:408

commit v4 on v3

--- a/solution.py
+++ b/solution.py
@@ -269,10 +269,8 @@
     odd_ref[...] = jnp.dot(to_ref[...], odd, preferred_element_type=jnp.float32)
 
 
-def combine(taps_ref, beam, even_ref, odd_ref, pack_ref, out_ref):
+def combine(taps_ref, beam, even_ref, odd_ref, pack_ref, signal_ref, out_ref):
     lane = lax.broadcasted_iota(jnp.int32, (ROWS, FR), 1)
-    slot = lane // 4
-    row = lax.rem(beam + LOCAL_BEAMS + 1, LOCAL_BEAMS + 1)
     for r in range(0, HALF, ROWS):
         cos_rows, sin_rows = pl.ds(r, ROWS), pl.ds(HALF + r, ROWS)
         parts = []
@@ -280,7 +278,6 @@
             real = ref[cos_rows, :FR] - ref[sin_rows, FR:]
             imag = ref[sin_rows, :FR] + ref[cos_rows, FR:]
             parts.append((real, imag))
-        packed = pack_ref[cos_rows, :]
         for n1 in range(2):
             rows = pl.ds(n1 * HALF + r, ROWS)
             for ri in range(2):
@@ -290,20 +287,27 @@
                 for k in range(1, TAPS):
                     shifted = jnp.where(lane >= k, pltpu.roll(signal, k, 1), 0.0)
                     total += taps_ref[k, rows, :] * shifted
-                out_ref[row, rows, ri * FR : (ri + 1) * FR] = total.astype(jnp.bfloat16)
-                where = beam * 4 + n1 * 2 + ri
-                packed = jnp.where(
-                    slot == where, pltpu.roll(signal, lax.rem(where * 4 + 4 + FR, FR), 1), packed
-                )
-        pack_ref[cos_rows, :] = packed
+                out_ref[beam, rows, ri * FR : (ri + 1) * FR] = total.astype(jnp.bfloat16)
+                signal_ref[n1, cos_rows, ri * FR : (ri + 1) * FR] = signal.astype(jnp.bfloat16)
+    source = lax.broadcasted_iota(jnp.int32, (2 * FR, FR), 0)
+    target = lax.broadcasted_iota(jnp.int32, (2 * FR, FR), 1)
+    frame, ri = source % FR - (FR - 4), source // FR
+    for n1 in range(2):
+        chosen = (frame >= 0) & (target == (beam * 4 + n1 * 2 + ri) * 4 + frame)
+        pack_ref[...] += jnp.dot(
+            signal_ref[n1],
+            jnp.where(chosen, 1.0, 0.0).astype(jnp.bfloat16),
+            preferred_element_type=jnp.float32,
+        )
 
 
 def synth_kernel(te_ref, to_ref, narrow_ref, y_ref, out_ref, tail_ref, *scratch):
-    buffers, (pack_ref, taps_ref) = (scratch[0:2], scratch[2:4]), scratch[4:]
+    buffers, (pack_ref, taps_ref, signal_ref) = (scratch[0:2], scratch[2:4]), scratch[4:]
     step = pl.program_id(0)
 
     @pl.when(step == 0)
     def _():
+        pack_ref[...] = jnp.zeros_like(pack_ref)
         narrow = narrow_ref[...]
         columns = jnp.transpose(jnp.concatenate([narrow, narrow], axis=0))
         for k in range(TAPS):
@@ -311,17 +315,26 @@
 
     last = pl.num_programs(0) - 1
 
-    def half(i):
-        done = 2 * step + i - 1
-        arriving = jnp.minimum(2 * step + i, LOCAL_BEAMS - 1)
-        transform(te_ref, to_ref, y_ref, arriving, *buffers[i])
-        combine(taps_ref, done, *buffers[1 - i], pack_ref, out_ref)
-
-    half(0)
+    def half(i, back=True):
+        transform(te_ref, to_ref, y_ref, 2 * step + i, *buffers[i])
+        if back:
+            combine(taps_ref, 2 * step + i - 1, *buffers[1 - i], pack_ref, signal_ref, out_ref)
+
+    @pl.when(step == 0)
+    def _():
+        half(0, back=False)
+
+    @pl.when((step > 0) & (step < last))
+    def _():
+        half(0)
 
     @pl.when(step < last)
     def _():
         half(1)
+
+    @pl.when(step == last)
+    def _():
+        combine(taps_ref, LOCAL_BEAMS - 1, *buffers[1], pack_ref, signal_ref, out_ref)
 
     @pl.when(step == last)
     def _():
@@ -349,11 +362,15 @@
         in_specs=[whole] * 4,
         out_specs=[whole, whole],
         out_shape=[
-            jax.ShapeDtypeStruct((LOCAL_BEAMS + 1, C, 2 * FR), jnp.bfloat16),
+            jax.ShapeDtypeStruct((LOCAL_BEAMS, C, 2 * FR), jnp.bfloat16),
             jax.ShapeDtypeStruct((HALF, FR), jnp.bfloat16),
         ],
         scratch_shapes=[product] * 4
-        + [pltpu.VMEM((HALF, FR), jnp.float32), pltpu.VMEM((TAPS, C, FR), jnp.float32)],
+        + [
+            pltpu.VMEM((HALF, FR), jnp.float32),
+            pltpu.VMEM((TAPS, C, FR), jnp.float32),
+            pltpu.VMEM((2, HALF, 2 * FR), jnp.bfloat16),
+        ],
         compiler_params=pltpu.CompilerParams(vmem_limit_bytes=SYNTH_VMEM),
         name="synthesis",
     )(jnp.asarray(parity_table(0)), jnp.asarray(parity_table(1)), filter_taps, received)

time: 204 us -> 201 us (0.985)
  Pallas kernels: 37.6 us -> 34.6 us
    pallas_call x1, Pallas kernels: 11.8 us -> 8.79 us  [synthesize(): pl.pallas_call(synth_kernel, grid=(steps,), in_specs=[whole] * 4, out_spe...]
where the time goes in v4:
time: 201 us
  blocking collectives  157 us (78%)
  Pallas kernels  34.6 us (17%)
  waiting for transfers between devices  5.92 us (3%)
  starting transfers between devices  2.94 us (1%)
    all_to_all x1, blocking collectives, per_device(): lax.all_to_all(turned, 'chan', split_axis=0, concat_axis=0, tiled=True)  103 us
    all_to_all x1, blocking collectives, per_device(): lax.all_to_all(beamed, 'chan', split_axis=0, concat_axis=0, tiled=True)  54.5 us
    pallas_call x1, Pallas kernels, form_beams(): pl.pallas_call(beam_kernel, in_specs=[pl.BlockSpec(memory_space=pltpu.SME...  15.3 us
    pallas_call x1, Pallas kernels, synthesize(): pl.pallas_call(synth_kernel, grid=(steps,), in_specs=[whole] * 4, out_spe...  8.79 us
    pallas_call x1, Pallas kernels, scale_and_turn(): pl.pallas_call(scale_kernel, in_specs=[pl.BlockSpec(memory_space=pltpu.SM...  7.71 us
    ppermute x1, waiting for transfers between devices, per_device(): incoming = lax.ppermute(tail, 'tm', [(g, g + 1) for g in range(groups - 1)])  5.92 us
  transfers between devices with their start and end apart: 1, of which 1 were waited for; matrix products, arithmetic and copies ran while one was open for 0% of the time, Pallas kernels for 0%

profile of v4, /device:TPU:128, one launch (start us, length us, event | category | flops | bytes accessed | tf_op | source)
XLA Modules:
  0.0 201.0 jit_solution(263445992291605504)
XLA Ops:
  0.0 7.7 %scale.1 = bf16[1024,16,256]{2,1,0:T(8,128)(2,1)} custom-call(s32[16,16]{1,0:T(8,128)} %bitcast.10, bf16[16,1024,256]{2,1,0:T(8,128)(2,1)} %volt_hbm.1), custom_call_target="tpu_custom_call" | custom-call | tf_op jit(solution)/shard_map/scale/pallas_call | solution.py:97
  7.7 0.0 copy-start.2
  7.7 0.0 copy-start.3
  7.7 0.0 copy-start.4
  7.8 102.9 %all_to_all.10 = bf16[1024,16,256]{2,1,0:T(8,128)(2,1)S(1)} all-to-all(bf16[1024,16,256]{2,1,0:T(8,128)(2,1)} %scale.1), channel_id=1, replica_groups=mesh['tm'=8,'chan'=32] {'chan'}, dimensions={0} | all-to-all | bytes 16777216 | tf_op jit(solution)/shard_map/all_to_all | solution.py:418
  110.7 0.0 copy-done.2
  110.7 0.0 copy-done.3
  110.7 0.0 copy-done.4
  110.7 15.3 %beamform.1 = bf16[256,2,16,256]{3,2,1,0:T(8,128)(2,1)S(1)} custom-call(s32[1]{0:T(128)} %bitcast.1.start_ref, f32[32,512]{1,0:T(8,128)S(1)} %bitcast.8, f32[32,512]{1,0:T(8,128)S(1)} %bitcast.9, f32[512,256]{1,0:T(8,128)S(1)} %copy-done.2, bf16[32,16,2,16,256]{4,3,2,1,0:T(8,128)(2,1)S(1)} %bitcast.6), custom_call_target="tpu_custom_call" | custom-call | tf_op jit(solution)/shard_map/beamform/pallas_call | solution.py:235
  126.0 0.0 copy-start
  126.1 0.0 copy-start.1
  126.1 0.0 copy-start.5
  126.1 54.5 %all_to_all.11 = bf16[256,2,16,256]{3,2,1,0:T(8,128)(2,1)S(1)} all-to-all(bf16[256,2,16,256]{3,2,1,0:T(8,128)(2,1)S(1)} %beamform.1), channel_id=1, replica_groups=mesh['tm'=8,'chan'=32] {'chan'}, dimensions={0} | all-to-all | bytes 8388608 | tf_op jit(solution)/shard_map/all_to_all | solution.py:422
  180.6 0.0 copy-done
  180.6 0.0 copy-done.1
  180.6 0.0 copy-done.5
  180.6 8.8 %synthesis.1 = (bf16[8,1024,256]{2,1,0:T(8,128)(2,1)S(1)}, bf16[512,128]{1,0:T(8,128)(2,1)S(1)}) custom-call(bf16[1024,512]{1,0:T(8,128)(2,1)S(1)} %copy-done.1, bf16[1024,512]{1,0:T(8,128)(2,1)S(1)} %copy-done, f32[4,1024]{1,0:T(4,128)S(1)} %copy-done.5, bf16[32,8,2,16,256]{4,3,2,1,0:T(8,128)(2,1)S(1)} %bitcast.7), custom_call_target="tpu_custom_call" | custom-call | tf_op jit(solution)/shard_map/synthesis/pallas_call | solution.py:359
  189.4 2.9 %collective-permute-start = (bf16[512,128]{1,0:T(8,128)(2,1)S(1)}, bf16[512,128]{1,0:T(8,128)(2,1)S(1)}, u32[]{:S(2)}, u32[]{:S(2)}) collective-permute-start(bf16[512,128]{1,0:T(8,128)(2,1)S(1)} %get-tuple-element.11), channel_id=1, source_target_pairs={{0,32},{32,64},{64,96},{96,128},{128,160},{160,192},{192,224},{1,3... | collective-permute-start | bytes 393224 | tf_op jit(solution)/shard_map/ppermute | solution.py:425
  192.3 5.9 %collective-permute-done.in_ref = bf16[512,128]{1,0:T(8,128)(2,1)S(1)} collective-permute-done((bf16[512,128]{1,0:T(8,128)(2,1)S(1)}, bf16[512,128]{1,0:T(8,128)(2,1)S(1)}, u32[]{:S(2)}, u32[]{:S(2)}) %collective-permute-start) | collective-permute-done | bytes 131104 | tf_op jit(solution)/shard_map/ppermute | solution.py:425
  198.3 2.8 %patch.1 = bf16[8,1024,256]{2,1,0:T(8,128)(2,1)} custom-call(bf16[512,128]{1,0:T(8,128)(2,1)S(1)} %collective-permute-done.in_ref, bf16[8,1024,256]{2,1,0:T(8,128)(2,1)S(1)} %get-tuple-element.12.series_ref), custom_call_target="tpu_custom_call" | custom-call | tf_op jit(solution)/shard_map/patch/pallas_call | solution.py:402
Async XLA Ops:
  7.7 103.0 %copy-start.2 = (f32[512,256]{1,0:T(8,128)S(1)}, f32[512,256]{1,0:T(8,128)}, u32[]{:S(2)}) copy-start(f32[512,256]{1,0:T(8,128)} %delay_ref.1) | copy-start | bytes 1572868
  7.7 103.0 %copy-start.3 = (f32[512,32]{0,1:T(8,128)S(1)}, f32[512,32]{0,1:T(8,128)}, u32[]{:S(2)}) copy-start(f32[512,32]{0,1:T(8,128)} %param.10) | copy-start | bytes 196612
  7.7 102.9 %copy-start.4 = (f32[512,32]{0,1:T(8,128)S(1)}, f32[512,32]{0,1:T(8,128)}, u32[]{:S(2)}) copy-start(f32[512,32]{0,1:T(8,128)} %param.11) | copy-start | bytes 196612
  126.0 54.5 %copy-start = (bf16[1024,512]{1,0:T(8,128)(2,1)S(1)}, bf16[1024,512]{1,0:T(8,128)(2,1)}, u32[]{:S(2)}) copy-start(bf16[1024,512]{1,0:T(8,128)(2,1)} %constant.11.clone.to_ref) | copy-start | bytes 3145732
  126.1 54.5 %copy-start.1 = (bf16[1024,512]{1,0:T(8,128)(2,1)S(1)}, bf16[1024,512]{1,0:T(8,128)(2,1)}, u32[]{:S(2)}) copy-start(bf16[1024,512]{1,0:T(8,128)(2,1)} %constant.10.clone.te_ref) | copy-start | bytes 3145732
  126.1 54.5 %copy-start.5 = (f32[4,1024]{1,0:T(4,128)S(1)}, f32[4,1024]{1,0:T(4,128)}, u32[]{:S(2)}) copy-start(f32[4,1024]{1,0:T(4,128)} %narrow_ref.1) | copy-start | bytes 49156
  189.4 8.9 %collective-permute-start = (bf16[512,128]{1,0:T(8,128)(2,1)S(1)}, bf16[512,128]{1,0:T(8,128)(2,1)S(1)}, u32[]{:S(2)}, u32[]{:S(2)}) collective-permute-start(bf16[512,128]{1,0:T(8,128)(2,1)S(1)} %get-tuple-element.11), channel_id=1, source_target_pairs={{0,32},{32,64},{64,96},{96,128},{128,160},{160,192},{192,224},{1,3... | collective-permute-start | bytes 393224 | tf_op jit(solution)/shard_map/ppermute | solution.py:425

commit v5 on v4

--- a/solution.py
+++ b/solution.py
@@ -14,7 +14,7 @@
 TILE = 16
 FR = 128
 TWO_PI = 6.283185307179586
-VMEM_MOST = 60 * 2**20
+SCALE_VMEM = 44 * 2**20
 SYNTH_VMEM = 32 * 2**20
 BEAM_VMEM = 36 * 2**20
 
@@ -56,14 +56,10 @@
 CB = 64
 
 
-def scale_kernel(exp_ref, volt_hbm, out_hbm, volt_ref, out_ref, perm_ref, in_sems, out_sems):
+def scale_kernel(exp_ref, volt_hbm, out_ref, volt_ref, perm_ref, in_sems):
     def arrival(j):
         part = pl.ds(j * SC_STEP, SC_STEP)
         return pltpu.make_async_copy(volt_hbm.at[:, part], volt_ref.at[:, part], in_sems.at[j])
-
-    def departure(j):
-        part = pl.ds(j * SC_STEP, SC_STEP)
-        return pltpu.make_async_copy(out_ref.at[part], out_hbm.at[part], out_sems.at[j])
 
     steps = C // SC_STEP
     for j in range(steps):
@@ -84,12 +80,9 @@
                 moved = jnp.dot(perm_ref[...], rows, preferred_element_type=jnp.float32)
                 scaled = moved.reshape(TILE, TILE, 2 * FR) * factor[None]
                 out_ref[pl.ds(start, TILE)] = scaled.astype(jnp.bfloat16)
-        departure(j).start()
         return carry
 
     lax.fori_loop(0, steps, scale, 0)
-    for j in range(steps):
-        departure(j).wait()
 
 
 def scale_and_turn(voltages, exponents):
@@ -97,16 +90,14 @@
     return pl.pallas_call(
         scale_kernel,
         in_specs=[pl.BlockSpec(memory_space=pltpu.SMEM), remote],
-        out_specs=remote,
+        out_specs=pl.BlockSpec(memory_space=pltpu.VMEM),
         out_shape=jax.ShapeDtypeStruct((C, TILE, 2 * FR), jnp.bfloat16),
         scratch_shapes=[
             pltpu.VMEM((TILE, C, 2 * FR), jnp.bfloat16),
-            pltpu.VMEM((C, TILE, 2 * FR), jnp.bfloat16),
             pltpu.VMEM((256, 256), jnp.bfloat16),
             pltpu.SemaphoreType.DMA((C // SC_STEP,)),
-            pltpu.SemaphoreType.DMA((C // SC_STEP,)),
         ],
-        compiler_params=pltpu.CompilerParams(vmem_limit_bytes=VMEM_MOST),
+        compiler_params=pltpu.CompilerParams(vmem_limit_bytes=SCALE_VMEM),
         name="scale",
     )(exponents, voltages)
 
@@ -122,7 +113,6 @@
     gi_ref,
     delay_ref,
     x_ref,
-    out_hbm,
     out_ref,
     beams_even,
     beams_odd,
@@ -135,11 +125,7 @@
     pi_ref,
     two_ref,
     gain_ref,
-    out_sems,
 ):
-    def departure(q):
-        return pltpu.make_async_copy(out_ref.at[q], out_hbm.at[:, q], out_sems.at[q])
-
     beams_refs = (beams_even, beams_odd)
     perm_ref[...] = swap_matrix()
 
@@ -200,7 +186,7 @@
         part = pl.ds(pl.multiple_of(group * TILE, TILE), TILE)
         rows = beams_refs[q][:, part, :].reshape(256, 2 * FR)
         moved = jnp.dot(perm_ref[...], rows, preferred_element_type=jnp.float32)
-        out_ref[q, part] = moved.reshape(TILE, TILE, 2 * FR).astype(jnp.bfloat16)
+        out_ref[part, q] = moved.reshape(TILE, TILE, 2 * FR).astype(jnp.bfloat16)
 
     groups = BEAMS // TILE
     for block in range(STATIONS // 128):
@@ -219,13 +205,8 @@
             return carry
 
         lax.fori_loop(0, CHUNKS // 2, pair, 0)
-        if q == 1:
-            departure(0).start()
     for group in range(groups):
         turn(1, group)
-    departure(1).start()
-    for q in range(2):
-        departure(q).wait()
 
 
 def form_beams(chan_start, gain_real, gain_imag, delays, received):
@@ -235,10 +216,9 @@
     return pl.pallas_call(
         beam_kernel,
         in_specs=[pl.BlockSpec(memory_space=pltpu.SMEM), whole, whole, whole, whole],
-        out_specs=pl.BlockSpec(memory_space=pl.ANY),
+        out_specs=whole,
         out_shape=jax.ShapeDtypeStruct((BEAMS, 2, TILE, 2 * FR), jnp.bfloat16),
         scratch_shapes=[
-            pltpu.VMEM((2, BEAMS, TILE, 2 * FR), jnp.bfloat16),
             pltpu.VMEM((16, BEAMS, 2 * FR), jnp.bfloat16),
             pltpu.VMEM((16, BEAMS, 2 * FR), jnp.bfloat16),
             pltpu.VMEM((256, 256), jnp.bfloat16),
@@ -250,7 +230,6 @@
             phasor,
             pltpu.VMEM((BEAMS, STATIONS), jnp.float32),
             pltpu.VMEM((2, gain_real.shape[0], 1, STATIONS), jnp.float32),
-            pltpu.SemaphoreType.DMA((2,)),
         ],
         compiler_params=pltpu.CompilerParams(vmem_limit_bytes=BEAM_VMEM),
         name="beamform",

time: 201 us -> 199 us (0.990)
  Pallas kernels: 34.6 us -> 31.9 us
    pallas_call x1, Pallas kernels: 7.71 us -> 5.51 us  [scale_and_turn(): pl.pallas_call(scale_kernel, in_specs=[pl.BlockSpec(memory_space=pltpu.SM...]
where the time goes in v5:
time: 199 us
  blocking collectives  157 us (79%)
  Pallas kernels  31.9 us (16%)
  waiting for transfers between devices  5.92 us (3%)
  starting transfers between devices  2.94 us (1%)
    all_to_all x1, blocking collectives, per_device(): lax.all_to_all(turned, 'chan', split_axis=0, concat_axis=0, tiled=True)  103 us
    all_to_all x1, blocking collectives, per_device(): lax.all_to_all(beamed, 'chan', split_axis=0, concat_axis=0, tiled=True)  54.5 us
    pallas_call x1, Pallas kernels, form_beams(): pl.pallas_call(beam_kernel, in_specs=[pl.BlockSpec(memory_space=pltpu.SME...  14.8 us
    pallas_call x1, Pallas kernels, synthesize(): pl.pallas_call(synth_kernel, grid=(steps,), in_specs=[whole] * 4, out_spe...  8.79 us
    ppermute x1, waiting for transfers between devices, per_device(): incoming = lax.ppermute(tail, 'tm', [(g, g + 1) for g in range(groups - 1)])  5.92 us
    pallas_call x1, Pallas kernels, scale_and_turn(): pl.pallas_call(scale_kernel, in_specs=[pl.BlockSpec(memory_space=pltpu.SM...  5.51 us
  transfers between devices with their start and end apart: 1, of which 1 were waited for; matrix products, arithmetic and copies ran while one was open for 0% of the time, Pallas kernels for 0%

profile of v5, /device:TPU:128, one launch (start us, length us, event | category | flops | bytes accessed | tf_op | source)
XLA Modules:
  0.0 198.8 jit_solution(11633267077348091539)
XLA Ops:
  0.0 0.0 copy-start.6
  0.0 0.7 copy-done.6
  0.7 5.5 %scale.1 = bf16[1024,16,256]{2,1,0:T(8,128)(2,1)S(1)} custom-call(s32[16,16]{1,0:T(8,128)S(1)} %bitcast.10, bf16[16,1024,256]{2,1,0:T(8,128)(2,1)} %volt_hbm.1), custom_call_target="tpu_custom_call" | custom-call | tf_op jit(solution)/shard_map/scale/pallas_call | solution.py:90
  6.2 0.0 copy-start.2
  6.2 0.0 copy-start.3
  6.2 0.0 copy-start.4
  6.2 102.7 %all_to_all.10 = bf16[1024,16,256]{2,1,0:T(8,128)(2,1)S(1)} all-to-all(bf16[1024,16,256]{2,1,0:T(8,128)(2,1)S(1)} %scale.1), channel_id=1, replica_groups=mesh['tm'=8,'chan'=32] {'chan'}, dimensions={0} | all-to-all | bytes 16777216 | tf_op jit(solution)/shard_map/all_to_all | solution.py:397
  109.0 0.0 copy-done.2
  109.0 0.0 copy-done.3
  109.0 0.0 copy-done.4
  109.0 14.8 %beamform.1 = bf16[256,2,16,256]{3,2,1,0:T(8,128)(2,1)S(1)} custom-call(s32[1]{0:T(128)} %bitcast.1.start_ref, f32[32,512]{1,0:T(8,128)S(1)} %bitcast.8, f32[32,512]{1,0:T(8,128)S(1)} %bitcast.9, f32[512,256]{1,0:T(8,128)S(1)} %copy-done.2, bf16[32,16,2,16,256]{4,3,2,1,0:T(8,128)(2,1)S(1)} %bitcast.6), custom_call_target="tpu_custom_call" | custom-call | tf_op jit(solution)/shard_map/beamform/pallas_call | solution.py:216
  123.8 0.0 copy-start
  123.8 0.0 copy-start.1
  123.8 0.0 copy-start.5
  123.8 54.5 %all_to_all.11 = bf16[256,2,16,256]{3,2,1,0:T(8,128)(2,1)S(1)} all-to-all(bf16[256,2,16,256]{3,2,1,0:T(8,128)(2,1)S(1)} %beamform.1), channel_id=1, replica_groups=mesh['tm'=8,'chan'=32] {'chan'}, dimensions={0} | all-to-all | bytes 8388608 | tf_op jit(solution)/shard_map/all_to_all | solution.py:401
  178.3 0.0 copy-done
  178.3 0.0 copy-done.1
  178.3 0.0 copy-done.5
  178.3 8.8 %synthesis.1 = (bf16[8,1024,256]{2,1,0:T(8,128)(2,1)S(1)}, bf16[512,128]{1,0:T(8,128)(2,1)S(1)}) custom-call(bf16[1024,512]{1,0:T(8,128)(2,1)S(1)} %copy-done.1, bf16[1024,512]{1,0:T(8,128)(2,1)S(1)} %copy-done, f32[4,1024]{1,0:T(4,128)S(1)} %copy-done.5, bf16[32,8,2,16,256]{4,3,2,1,0:T(8,128)(2,1)S(1)} %bitcast.7), custom_call_target="tpu_custom_call" | custom-call | tf_op jit(solution)/shard_map/synthesis/pallas_call | solution.py:338
  187.1 2.9 %collective-permute-start = (bf16[512,128]{1,0:T(8,128)(2,1)S(1)}, bf16[512,128]{1,0:T(8,128)(2,1)S(1)}, u32[]{:S(2)}, u32[]{:S(2)}) collective-permute-start(bf16[512,128]{1,0:T(8,128)(2,1)S(1)} %get-tuple-element.11), channel_id=1, source_target_pairs={{0,32},{32,64},{64,96},{96,128},{128,160},{160,192},{192,224},{1,3... | collective-permute-start | bytes 393224 | tf_op jit(solution)/shard_map/ppermute | solution.py:404
  190.1 5.9 %collective-permute-done.in_ref = bf16[512,128]{1,0:T(8,128)(2,1)S(1)} collective-permute-done((bf16[512,128]{1,0:T(8,128)(2,1)S(1)}, bf16[512,128]{1,0:T(8,128)(2,1)S(1)}, u32[]{:S(2)}, u32[]{:S(2)}) %collective-permute-start) | collective-permute-done | bytes 131104 | tf_op jit(solution)/shard_map/ppermute | solution.py:404
  196.0 2.8 %patch.1 = bf16[8,1024,256]{2,1,0:T(8,128)(2,1)} custom-call(bf16[512,128]{1,0:T(8,128)(2,1)S(1)} %collective-permute-done.in_ref, bf16[8,1024,256]{2,1,0:T(8,128)(2,1)S(1)} %get-tuple-element.12.series_ref), custom_call_target="tpu_custom_call" | custom-call | tf_op jit(solution)/shard_map/patch/pallas_call | solution.py:381
Async XLA Ops:
  0.0 0.7 copy-start.6
  6.2 102.7 %copy-start.2 = (f32[512,256]{1,0:T(8,128)S(1)}, f32[512,256]{1,0:T(8,128)}, u32[]{:S(2)}) copy-start(f32[512,256]{1,0:T(8,128)} %delay_ref.1) | copy-start | bytes 1572868
  6.2 102.7 %copy-start.3 = (f32[512,32]{0,1:T(8,128)S(1)}, f32[512,32]{0,1:T(8,128)}, u32[]{:S(2)}) copy-start(f32[512,32]{0,1:T(8,128)} %param.10) | copy-start | bytes 196612
  6.2 102.7 %copy-start.4 = (f32[512,32]{0,1:T(8,128)S(1)}, f32[512,32]{0,1:T(8,128)}, u32[]{:S(2)}) copy-start(f32[512,32]{0,1:T(8,128)} %param.11) | copy-start | bytes 196612
  123.8 54.5 %copy-start = (bf16[1024,512]{1,0:T(8,128)(2,1)S(1)}, bf16[1024,512]{1,0:T(8,128)(2,1)}, u32[]{:S(2)}) copy-start(bf16[1024,512]{1,0:T(8,128)(2,1)} %constant.11.clone.to_ref) | copy-start | bytes 3145732
  123.8 54.5 %copy-start.1 = (bf16[1024,512]{1,0:T(8,128)(2,1)S(1)}, bf16[1024,512]{1,0:T(8,128)(2,1)}, u32[]{:S(2)}) copy-start(bf16[1024,512]{1,0:T(8,128)(2,1)} %constant.10.clone.te_ref) | copy-start | bytes 3145732
  123.8 54.5 %copy-start.5 = (f32[4,1024]{1,0:T(4,128)S(1)}, f32[4,1024]{1,0:T(4,128)}, u32[]{:S(2)}) copy-start(f32[4,1024]{1,0:T(4,128)} %narrow_ref.1) | copy-start | bytes 49156
  187.1 8.9 %collective-permute-start = (bf16[512,128]{1,0:T(8,128)(2,1)S(1)}, bf16[512,128]{1,0:T(8,128)(2,1)S(1)}, u32[]{:S(2)}, u32[]{:S(2)}) collective-permute-start(bf16[512,128]{1,0:T(8,128)(2,1)S(1)} %get-tuple-element.11), channel_id=1, source_target_pairs={{0,32},{32,64},{64,96},{96,128},{128,160},{160,192},{192,224},{1,3... | collective-permute-start | bytes 393224 | tf_op jit(solution)/shard_map/ppermute | solution.py:404
